TPU v7x, 512 devices: a whole 4x8x8 slice. The times are simulated.
512 devices in a mesh: req: 16 (over y, core), cand: 32 (over x, z).
Axes of the slice: x: 4, y: 8, z: 8, core: 2. Of those that a mesh axis runs over, the one named last changes fastest.
Arguments:
- cand_rows: bfloat16 [16, 16384, 512], P('req', 'cand'), may hold values from -6 to 6
- user_rows: bfloat16 [16, 64, 512], P('req', 'cand'), may hold values from -6 to 6
- row_owner: int32 [16, 16384, 1], P('req', 'cand'), may hold values from 0 to 31; in each aligned block of 512 rows (0 to 511, 512 to 1023, ..., all dimensions but the last counted through in order) at most 32 rows name the same one
- row_list: int32 [16, 16384], P('req', 'cand'), may hold values from 0 to 1
- cross_weight: bfloat16 [512, 512], replicated, may hold values from -0.25 to 0.25
- up_weight: bfloat16 [512, 1024], replicated, may hold values from -0.25 to 0.25
- down_weight: bfloat16 [1024, 512], replicated, may hold values from -0.1875 to 0.1875
- project_in: bfloat16 [512, 1536], P('req'), may hold values from -0.25 to 0.25
- project_out: bfloat16 [512, 512], replicated, may hold values from -0.25 to 0.25
Outputs:
- reranked: bfloat16 [16, 16384, 512], P('req', 'cand')
Inputs may be any that keep to these rules, and one draw needn't show every extreme that they name: `row_owner`: among the rows of one device, at most 32 name the same owner, and some device of every draw has an owner named exactly 32 times.
All inputs are finite; a program needn't handle non-finite values.
Results may differ from a plain program's by a relative error of at most 0.0068.
Values may be sent and summed in bfloat16 or wider, within the bound.
No kernel may reach another device: no remote copies, remote signals or barrier semaphores. Data moves between devices by JAX's collectives and lax.ppermute only.
A program may use at most 64 MiB of HBM per device.

v0:
```python
import jax
import jax.numpy as jnp
from jax import lax
from jax.sharding import PartitionSpec as P

HEADS = 8


def layers(combined, cross_weight, up_weight, down_weight):
    wide = combined.astype(jnp.float32)
    crossed = (
        wide * jnp.dot(combined, cross_weight, preferred_element_type=jnp.float32) + wide
    ).astype(jnp.bfloat16)
    activated = jax.nn.relu(jnp.dot(crossed, up_weight, preferred_element_type=jnp.float32)).astype(
        jnp.bfloat16
    )
    return (
        crossed.astype(jnp.float32)
        + jnp.dot(activated, down_weight, preferred_element_type=jnp.float32)
    ).astype(jnp.bfloat16)


def add_users(rows_here, user_table, user_index):
    table_rows = user_table.shape[0]
    select = (user_index[:, None] == jnp.arange(table_rows, dtype=jnp.int32)[None, :]).astype(
        jnp.bfloat16
    )
    picked = jnp.dot(select, user_table, preferred_element_type=jnp.float32)
    return (rows_here.astype(jnp.float32) + picked).astype(jnp.bfloat16)


def project(mixed_rows, project_in):
    buffer_rows, model_width = mixed_rows.shape
    projected = jnp.dot(mixed_rows, project_in, preferred_element_type=jnp.float32)

    def normed(block):
        split = block.reshape(buffer_rows, HEADS, model_width // HEADS)
        split = split * lax.rsqrt(jnp.mean(split * split, axis=-1, keepdims=True) + 1e-06)
        return split.reshape(buffer_rows, model_width).astype(jnp.bfloat16)

    queries = normed(projected[:, :model_width])
    keys_all = normed(projected[:, model_width : 2 * model_width])
    values_all = projected[:, 2 * model_width :].astype(jnp.bfloat16)
    return (queries, keys_all, values_all)


def attend(mixed_rows, queries, keys_all, values_all, list_tags, project_out):
    buffer_rows, model_width = mixed_rows.shape
    head_width = model_width // HEADS
    score_scale = head_width ** (-0.5)
    same_list = list_tags[:, None] == list_tags[None, :]

    def one_head(head_index):
        start = head_index * head_width
        query_part = lax.dynamic_slice_in_dim(queries, start, head_width, 1)
        key_part = lax.dynamic_slice_in_dim(keys_all, start, head_width, 1)
        value_part = lax.dynamic_slice_in_dim(values_all, start, head_width, 1)
        scores = jnp.dot(query_part, key_part.T, preferred_element_type=jnp.float32) * score_scale
        powered = jnp.where(same_list, jnp.exp(scores), jnp.float32(0.0))
        weights = (powered / jnp.sum(powered, axis=1, keepdims=True)).astype(jnp.bfloat16)
        return jnp.dot(weights, value_part, preferred_element_type=jnp.float32).astype(jnp.bfloat16)

    per_head = lax.map(one_head, jnp.arange(HEADS, dtype=jnp.int32))
    attended = per_head.transpose(1, 0, 2).reshape(buffer_rows, model_width)
    return (
        mixed_rows.astype(jnp.float32)
        + jnp.dot(attended, project_out, preferred_element_type=jnp.float32)
    ).astype(jnp.bfloat16)


def local(
    cand_rows,
    user_rows,
    row_owner,
    row_list,
    cross_weight,
    up_weight,
    down_weight,
    project_in,
    project_out,
):
    inward = lax.all_gather(project_in, "req", axis=0, tiled=True)
    rows_here = cand_rows[0]
    owner_ids = row_owner[0, :, 0]
    list_ids = row_list[0]
    peer_count = lax.axis_size("cand")
    local_rows = rows_here.shape[0]
    model_width = rows_here.shape[1]
    capacity = 2 * local_rows // peer_count
    onehot = (owner_ids[:, None] == jnp.arange(peer_count, dtype=jnp.int32)[None, :]).astype(
        jnp.int32
    )
    slot_rank = jnp.sum(jnp.cumsum(onehot, axis=0) * onehot, axis=1) - 1
    position = owner_ids * capacity + slot_rank
    tags_here = list_ids + 1

    def outgoing(values):
        empty = jnp.zeros((peer_count * capacity,) + values.shape[1:], values.dtype)
        return empty.at[position].set(values).reshape((peer_count, capacity) + values.shape[1:])

    user_table = lax.all_gather(user_rows[0], "cand", axis=0, tiled=True)
    local_mixed = layers(
        add_users(rows_here, user_table, owner_ids * user_rows.shape[1] + list_ids),
        cross_weight,
        up_weight,
        down_weight,
    )
    incoming, tags_in = (
        lax.all_to_all(outgoing(local_mixed), "cand", split_axis=0, concat_axis=0, tiled=True),
        lax.all_to_all(outgoing(tags_here), "cand", split_axis=0, concat_axis=0, tiled=True),
    )
    mixed_rows = incoming.reshape(-1, model_width)
    tags_flat = tags_in.reshape(-1)
    queries, keys_all, values_all = project(mixed_rows, inward)
    result = attend(mixed_rows, queries, keys_all, values_all, tags_flat, project_out)
    returned = lax.all_to_all(
        result.reshape(peer_count, capacity, model_width),
        "cand",
        split_axis=0,
        concat_axis=0,
        tiled=True,
    )
    return returned.reshape(-1, model_width)[position][None]


def solution(mesh):
    in_specs = (
        P("req", "cand", None),
        P("req", "cand", None),
        P("req", "cand", None),
        P("req", "cand"),
        P(),
        P(),
        P(),
        P("req", None),
        P(),
    )
    out_specs = P("req", "cand", None)
    return jax.shard_map(local, mesh=mesh, in_specs=in_specs, out_specs=out_specs, check_vma=False)
```

profile of v0, /device:TPU:24, one launch (start us, length us, event | category | flops | bytes accessed | tf_op | source)
XLA Modules:
  0.0 227.4 jit_solution(8071933101016540917)
XLA Ops:
  11.7 2.4 %scatter_custom_fusion.1 = s32[1024]{0:T(1024)S(1)} fusion(s32[512]{0:T(512)S(1)} %bitcast.70, s32[512]{0:T(512)S(1)} %get-tuple-element.80, s32[]{:T(128)} %constant.12.clone.1), kind=kCustom, calls=%fused_computation.54 | custom fusion | bytes 4100 | tf_op jit(solution)/shard_map/scatter | solution.py:99
  14.8 13.2 %all-to-all-start.1 = ((s32[32,1,32]{2,1,0:T(1,128)}), s32[32,1,32]{2,1,0:T(1,128)S(1)}, u32[]{:S(2)}, u32[]{:S(2)}) async-start(s32[32,1,32]{2,1,0:T(1,128)} %all_to_all.13), calls=%async_computation.1 | async-start | bytes 32768 | tf_op jit(solution)/shard_map/all_to_all | solution.py:110
  28.7 43.9 %all-gather = bf16[1,64,512]{2,0,1:T(2,128)(2,1)S(1)} all-gather(bf16[1,2,512]{2,0,1:T(2,128)(2,1)S(1)} %copy.22), channel_id=2, replica_groups=mesh['req'=16,'cand'=32] {'cand'}, dimensions={1}, use_global_device_ids=true | all-gather | bytes 67584 | tf_op jit(solution)/shard_map/all_gather | solution.py:101
  74.0 2.3 %fusion.17 = bf16[512,512]{1,0:T(8,128)(2,1)} fusion(bf16[512,512]{1,0:T(8,128)(2,1)S(1)} %fusion.15, bf16[512,512]{1,0:T(8,128)(2,1)} %param.15), kind=kOutput, calls=%fused_computation.33 | convolution fusion | flops 269484032 | bytes 1572864 | tf_op jit(solution)/shard_map/dot_general | solution.py:12
  76.2 2.5 %fusion.16 = bf16[512,512]{1,0:T(8,128)(2,1)S(1)} fusion(bf16[1024,512]{1,0:T(8,128)(2,1)S(1)} %copy-done, bf16[512,512]{1,0:T(8,128)(2,1)} %fusion.17, bf16[512,1024]{1,0:T(8,128)(2,1)S(1)} %copy-done.4), kind=kOutput, calls=%fused_computation.32 | convolution fusion | flops 1075576832 | bytes 3145728 | tf_op jit(solution)/shard_map/dot_general | solution.py:19
  78.7 3.5 %scatter_custom_fusion = bf16[1024,512]{1,0:T(8,128)(2,1)} fusion(s32[512]{0:T(512)S(1)} %bitcast.71, bf16[512,512]{1,0:T(8,128)(2,1)S(1)} %fusion.16, bf16[]{:T(256)} %constant.10.clone.1), kind=kCustom, calls=%fused_computation.35 | custom fusion | bytes 1048578 | tf_op jit(solution)/shard_map/scatter | solution.py:99
  82.2 7.2 %all-to-all-start = ((bf16[32,32,512]{2,1,0:T(8,128)(2,1)}), bf16[32,32,512]{2,1,0:T(8,128)(2,1)S(1)}, u32[]{:S(2)}, u32[]{:S(2)}) async-start(bf16[32,32,512]{2,1,0:T(8,128)(2,1)} %bitcast.8), calls=%async_computation | async-start | bytes 2097152 | tf_op jit(solution)/shard_map/all_to_all | solution.py:109
  90.7 19.1 %all-to-all-done = bf16[32,32,512]{2,1,0:T(8,128)(2,1)S(1)} async-done(((bf16[32,32,512]{2,1,0:T(8,128)(2,1)}), bf16[32,32,512]{2,1,0:T(8,128)(2,1)S(1)}, u32[]{:S(2)}, u32[]{:S(2)}) %all-to-all-start) | async-done | bytes 1048608 | tf_op jit(solution)/shard_map/all_to_all | solution.py:109
  109.8 3.6 %fusion.30 = f32[1024,1536]{1,0:T(8,128)S(1)} fusion(bf16[1024,512]{1,0:T(8,128)(2,1)S(1)} %bitcast.65, bf16[512,1536]{1,0:T(8,128)(2,1)} %all-gather.3.cloned.1.call-done), kind=kOutput, calls=%fused_computation.60 | convolution fusion | flops 1610612736 | bytes 8912896 | tf_op jit(solution)/shard_map/dot_general | solution.py:34
  113.4 2.9 %slice_multiply_fusion = (f32[1024,512]{1,0:T(8,128)}, f32[1024,512]{1,0:T(8,128)}) fusion(f32[1024,1536]{1,0:T(8,128)S(1)} %fusion.30), kind=kLoop, calls=%fused_computation.26 | loop fusion | flops 1048576 | bytes 8388608 | tf_op jit(solution)/shard_map/mul | solution.py:38
  124.3 3.0 %copy.25 = f32[1024,512]{0,1:T(8,128)} copy(f32[1024,512]{1,0:T(8,128)} %get-tuple-element.78) | data formatting | bytes 4194304 | tf_op jit(solution)/shard_map/mul | solution.py:38
  130.8 2.9 %copy.26 = f32[1024,512]{1,0:T(8,128)} copy(f32[1024,512]{0,1:T(8,128)} %bitcast.64) | data formatting | bytes 4194304 | tf_op jit(solution)/shard_map/mul | solution.py:38
  133.7 5.0 %multiply_convert_fusion = (bf16[1024,512]{1,0:T(8,128)(2,1)}, bf16[1024,512]{1,0:T(8,128)(2,1)}) fusion(f32[1024,512]{1,0:T(8,128)} %copy.26, f32[1024,1536]{1,0:T(8,128)} %copy-done.1, f32[1024,512]{1,0:T(8,128)S(1)} %copy.24), kind=kLoop, calls=%fused_computation.23 | loop fusion | flops 2097152 | bytes 10485760 | tf_op jit(solution)/shard_map/convert_element_type | solution.py:39
  138.7 50.3 %while.11 = (s32[]{:T(128)}, bf16[8,1024,64]{1,2,0:T(8,128)(2,1)}, s32[8]{0:T(128)S(1)}, bf16[1024,512]{1,0:T(8,128)(2,1)}, bf16[1024,512]{1,0:T(8,128)(2,1)}, /...) while((s32[]{:T(128)}, bf16[8,1024,64]{1,2,0:T(8,128)(2,1)}, ...), condition=%wide.region_9.10_spmd.clone, body=%wide.region_7.9_spmd.clone.sunk | while | flops 277937152 | bytes 9332395 | solution.py:63
  140.0 2.1 fusion.44
  142.2 2.8 %fusion.45 = bf16[8,1024,64]{1,2,0:T(8,128)(2,1)} fusion(bf16[8,1024,64]{1,2,0:T(8,128)(2,1)} %get-tuple-element.141, s32[]{:T(128)} %get-tuple-element.140, f32[1024,1024]{0,1:T(8,128)S(1)} %get-tuple-element.127, s32[1024]{0:T(1024)S(1)} %get-tuple-element.157, f32[1024]{0:T(1024)S(1)} %get-tuple-element.128, ...), kind=kOutput, calls=%fused_computation.10.clone.1 | convolution fusion | flops 139526144 | bytes 4600324 | tf_op jit(solution)/shard_map/while/body/eval_jaxpr/dot_general | solution.py:61
  146.3 2.1 fusion.44
  148.5 2.8 %fusion.45 = bf16[8,1024,64]{1,2,0:T(8,128)(2,1)} fusion(bf16[8,1024,64]{1,2,0:T(8,128)(2,1)} %get-tuple-element.141, s32[]{:T(128)} %get-tuple-element.140, f32[1024,1024]{0,1:T(8,128)S(1)} %get-tuple-element.127, s32[1024]{0:T(1024)S(1)} %get-tuple-element.157, f32[1024]{0:T(1024)S(1)} %get-tuple-element.128, ...), kind=kOutput, calls=%fused_computation.10.clone.1 | convolution fusion | flops 139526144 | bytes 4600324 | tf_op jit(solution)/shard_map/while/body/eval_jaxpr/dot_general | solution.py:61
  152.6 2.1 fusion.44
  154.8 2.8 %fusion.45 = bf16[8,1024,64]{1,2,0:T(8,128)(2,1)} fusion(bf16[8,1024,64]{1,2,0:T(8,128)(2,1)} %get-tuple-element.141, s32[]{:T(128)} %get-tuple-element.140, f32[1024,1024]{0,1:T(8,128)S(1)} %get-tuple-element.127, s32[1024]{0:T(1024)S(1)} %get-tuple-element.157, f32[1024]{0:T(1024)S(1)} %get-tuple-element.128, ...), kind=kOutput, calls=%fused_computation.10.clone.1 | convolution fusion | flops 139526144 | bytes 4600324 | tf_op jit(solution)/shard_map/while/body/eval_jaxpr/dot_general | solution.py:61
  158.9 2.1 fusion.44
  161.0 2.8 %fusion.45 = bf16[8,1024,64]{1,2,0:T(8,128)(2,1)} fusion(bf16[8,1024,64]{1,2,0:T(8,128)(2,1)} %get-tuple-element.141, s32[]{:T(128)} %get-tuple-element.140, f32[1024,1024]{0,1:T(8,128)S(1)} %get-tuple-element.127, s32[1024]{0:T(1024)S(1)} %get-tuple-element.157, f32[1024]{0:T(1024)S(1)} %get-tuple-element.128, ...), kind=kOutput, calls=%fused_computation.10.clone.1 | convolution fusion | flops 139526144 | bytes 4600324 | tf_op jit(solution)/shard_map/while/body/eval_jaxpr/dot_general | solution.py:61
  165.2 2.1 fusion.44
  167.3 2.8 %fusion.45 = bf16[8,1024,64]{1,2,0:T(8,128)(2,1)} fusion(bf16[8,1024,64]{1,2,0:T(8,128)(2,1)} %get-tuple-element.141, s32[]{:T(128)} %get-tuple-element.140, f32[1024,1024]{0,1:T(8,128)S(1)} %get-tuple-element.127, s32[1024]{0:T(1024)S(1)} %get-tuple-element.157, f32[1024]{0:T(1024)S(1)} %get-tuple-element.128, ...), kind=kOutput, calls=%fused_computation.10.clone.1 | convolution fusion | flops 139526144 | bytes 4600324 | tf_op jit(solution)/shard_map/while/body/eval_jaxpr/dot_general | solution.py:61
  173.6 2.8 %fusion.45 = bf16[8,1024,64]{1,2,0:T(8,128)(2,1)} fusion(bf16[8,1024,64]{1,2,0:T(8,128)(2,1)} %get-tuple-element.141, s32[]{:T(128)} %get-tuple-element.140, f32[1024,1024]{0,1:T(8,128)S(1)} %get-tuple-element.127, s32[1024]{0:T(1024)S(1)} %get-tuple-element.157, f32[1024]{0:T(1024)S(1)} %get-tuple-element.128, ...), kind=kOutput, calls=%fused_computation.10.clone.1 | convolution fusion | flops 139526144 | bytes 4600324 | tf_op jit(solution)/shard_map/while/body/eval_jaxpr/dot_general | solution.py:61
  177.7 2.1 fusion.44
  179.9 2.8 %fusion.45 = bf16[8,1024,64]{1,2,0:T(8,128)(2,1)} fusion(bf16[8,1024,64]{1,2,0:T(8,128)(2,1)} %get-tuple-element.141, s32[]{:T(128)} %get-tuple-element.140, f32[1024,1024]{0,1:T(8,128)S(1)} %get-tuple-element.127, s32[1024]{0:T(1024)S(1)} %get-tuple-element.157, f32[1024]{0:T(1024)S(1)} %get-tuple-element.128, ...), kind=kOutput, calls=%fused_computation.10.clone.1 | convolution fusion | flops 139526144 | bytes 4600324 | tf_op jit(solution)/shard_map/while/body/eval_jaxpr/dot_general | solution.py:61
  186.2 2.8 %fusion.45 = bf16[8,1024,64]{1,2,0:T(8,128)(2,1)} fusion(bf16[8,1024,64]{1,2,0:T(8,128)(2,1)} %get-tuple-element.141, s32[]{:T(128)} %get-tuple-element.140, f32[1024,1024]{0,1:T(8,128)S(1)} %get-tuple-element.127, s32[1024]{0:T(1024)S(1)} %get-tuple-element.157, f32[1024]{0:T(1024)S(1)} %get-tuple-element.128, ...), kind=kOutput, calls=%fused_computation.10.clone.1 | convolution fusion | flops 139526144 | bytes 4600324 | tf_op jit(solution)/shard_map/while/body/eval_jaxpr/dot_general | solution.py:61
  189.0 3.0 %add_convert_fusion = bf16[1024,512]{1,0:T(8,128)(2,1)} fusion(bf16[1024,512]{1,0:T(8,128)(2,1)S(1)} %bitcast.66, bf16[1024,512]{0,1:T(8,128)(2,1)} %bitcast.15, bf16[512,512]{1,0:T(8,128)(2,1)S(1)} %copy-done.5), kind=kOutput, calls=%fused_computation.22 | convolution fusion | flops 538443776 | bytes 3670016 | tf_op jit(solution)/shard_map/dot_general | solution.py:67
  191.9 5.4 %all-to-all-start.2 = ((bf16[32,32,512]{2,1,0:T(8,128)(2,1)}), bf16[32,32,512]{2,1,0:T(8,128)(2,1)S(1)}, u32[]{:S(2)}, u32[]{:S(2)}) async-start(bf16[32,32,512]{2,1,0:T(8,128)(2,1)} %bitcast.16), calls=%async_computation.2 | async-start | bytes 2097152 | tf_op jit(solution)/shard_map/all_to_all | solution.py:116
  197.3 20.5 %all-to-all-done.2 = bf16[32,32,512]{2,1,0:T(8,128)(2,1)S(1)} async-done(((bf16[32,32,512]{2,1,0:T(8,128)(2,1)}), bf16[32,32,512]{2,1,0:T(8,128)(2,1)S(1)}, u32[]{:S(2)}, u32[]{:S(2)}) %all-to-all-start.2) | async-done | bytes 1048608 | tf_op jit(solution)/shard_map/all_to_all | solution.py:116
  217.9 2.6 %gather_fusion = bf16[512,512]{1,0:T(8,128)(2,1)} fusion(bf16[1024,512]{1,0:T(8,128)(2,1)S(1)} %bitcast.62, s32[1024]{0:T(1024)S(1)} %pad_clamp_fusion), kind=kCustom, calls=%fused_computation | custom fusion | bytes 1050624 | tf_op jit(solution)/shard_map/gather | solution.py:123
  (53 shorter events, 30.2 us)
Async XLA Ops:
  6.5 69.7 %copy-start = (bf16[1024,512]{1,0:T(8,128)(2,1)S(1)}, bf16[1024,512]{1,0:T(8,128)(2,1)}, u32[]{:S(2)}) copy-start(bf16[1024,512]{1,0:T(8,128)(2,1)} %param.17) | copy-start | bytes 3145732
  6.5 103.2 %all-gather.3.cloned.1.call-start = ((), (), s32[]{:S(2)}) async-start(), calls=%async_computation.3 | async-start | bytes 1671168 | tf_op jit(solution)/shard_map/all_gather | solution.py:82
  10.2 66.1 %copy-start.4 = (bf16[512,1024]{1,0:T(8,128)(2,1)S(1)}, bf16[512,1024]{1,0:T(8,128)(2,1)}, u32[]{:S(2)}) copy-start(bf16[512,1024]{1,0:T(8,128)(2,1)} %param.16) | copy-start | bytes 3145732
  14.8 67.4 %all-to-all-start.1 = ((s32[32,1,32]{2,1,0:T(1,128)}), s32[32,1,32]{2,1,0:T(1,128)S(1)}, u32[]{:S(2)}, u32[]{:S(2)}) async-start(s32[32,1,32]{2,1,0:T(1,128)} %all_to_all.13), calls=%async_computation.1 | async-start | bytes 32768 | tf_op jit(solution)/shard_map/all_to_all | solution.py:110
  82.2 27.6 %all-to-all-start = ((bf16[32,32,512]{2,1,0:T(8,128)(2,1)}), bf16[32,32,512]{2,1,0:T(8,128)(2,1)S(1)}, u32[]{:S(2)}, u32[]{:S(2)}) async-start(bf16[32,32,512]{2,1,0:T(8,128)(2,1)} %bitcast.8), calls=%async_computation | async-start | bytes 2097152 | tf_op jit(solution)/shard_map/all_to_all | solution.py:109
  109.8 3.6 %copy-start.2 = (bf16[32,32,512]{2,1,0:T(8,128)(2,1)}, bf16[32,32,512]{2,1,0:T(8,128)(2,1)S(1)}, u32[]{:S(2)}) copy-start(bf16[32,32,512]{2,1,0:T(8,128)(2,1)S(1)} %all-to-all-done) | copy-start | bytes 3145732
  113.4 4.1 %copy-start.1 = (f32[1024,1536]{1,0:T(8,128)}, f32[1024,1536]{1,0:T(8,128)S(1)}, u32[]{:S(2)}) copy-start(f32[1024,1536]{1,0:T(8,128)S(1)} %fusion.30) | copy-start | bytes 18874372
  138.7 50.3 %copy-start.3 = (bf16[32,32,512]{2,1,0:T(8,128)(2,1)S(1)}, bf16[32,32,512]{2,1,0:T(8,128)(2,1)}, u32[]{:S(2)}) copy-start(bf16[32,32,512]{2,1,0:T(8,128)(2,1)} %copy-done.2) | copy-start | bytes 3145732
  138.7 50.3 %copy-start.5 = (bf16[512,512]{1,0:T(8,128)(2,1)S(1)}, bf16[512,512]{1,0:T(8,128)(2,1)}, u32[]{:S(2)}) copy-start(bf16[512,512]{1,0:T(8,128)(2,1)} %param.19) | copy-start | bytes 1572868
  191.9 26.0 %all-to-all-start.2 = ((bf16[32,32,512]{2,1,0:T(8,128)(2,1)}), bf16[32,32,512]{2,1,0:T(8,128)(2,1)S(1)}, u32[]{:S(2)}, u32[]{:S(2)}) async-start(bf16[32,32,512]{2,1,0:T(8,128)(2,1)} %bitcast.16), calls=%async_computation.2 | async-start | bytes 2097152 | tf_op jit(solution)/shard_map/all_to_all | solution.py:116
Sparse Core Ops, SparseCore 0:
  9.5 45.6 all-gather.2
where the time goes:
time: 229 us; the launch traced here: 227 us
  matrix products  52 us (23%)
  blocking collectives  43.9 us (19%)
  waiting for transfers between devices  40.4 us (18%)
  local copies, waits for them, and re-layouts  31.3 us (14%)
  starting transfers between devices  25.8 us (11%)
  other arithmetic  14.7 us (6%)
  between operations  13.6 us (6%)
  loops' own time  5.67 us (2%)
    all_gather x1, blocking collectives, local(): user_table = lax.all_gather(user_rows[0], 'cand', axis=0, tiled=True)  43.9 us
    dot_general x8, matrix products, one_head(): jnp.dot(weights, value_part, preferred_element_type=jnp.float32)  22.2 us
    all_to_all x1, waiting for transfers between devices, local(): lax.all_to_all(result.reshape(peer_count, capacity, model_width), 'cand',...  20.5 us
    all_to_all x1, waiting for transfers between devices, local(): lax.all_to_all(outgoing(local_mixed), 'cand', split_axis=0, concat_axis=0...  19.1 us
    dot_general x8, matrix products, one_head(): jnp.dot(query_part, key_part.T, preferred_element_type=jnp.float32)  17.1 us
    all_to_all x1, starting transfers between devices, local(): lax.all_to_all(outgoing(tags_here), 'cand', split_axis=0, concat_axis=0,...  13.2 us
    mul x4, local copies, waits for them, and re-layouts, normed(): split * lax.rsqrt(jnp.mean(split * split, axis=-1, keepdims=True) + 1e-06)  8.12 us
    all_to_all x1, starting transfers between devices, local(): lax.all_to_all(outgoing(local_mixed), 'cand', split_axis=0, concat_axis=0...  7.2 us
  transfers between devices with their start and end apart: 4, of which 2 were waited for; matrix products, arithmetic and copies ran while one was open for 8% of the time, Pallas kernels for 0%

commit v1 on v0

v1 whole, which is shorter than its diff:
```python
import jax
import jax.numpy as jnp
from jax import lax
from jax.experimental import pallas as pl
from jax.experimental.pallas import tpu as pltpu
from jax.sharding import PartitionSpec as P

HEADS = 8
PEERS = 32
CAP = 32
SLOTS = PEERS * CAP
D = 512
LANES = 128
COLS = D // LANES
PAY = COLS * CAP + 8
BLOCK = 256
APART = 1024.0
BF = jnp.bfloat16
F32 = jnp.float32
VMEM = pl.BlockSpec(memory_space=pltpu.VMEM)
NT = (((1,), (1,)), ((), ()))


def iota(shape, dim):
    return lax.broadcasted_iota(jnp.int32, shape, dim)


def ones_where(cond):
    return jnp.where(cond, 1.0, 0.0).astype(BF)


def dot(a, b):
    return jnp.dot(a, b, preferred_element_type=F32)


def pack_kernel(rows_ref, owner_ref, list_ref, pay_ref, pos_ref):
    rows = rows_ref.shape[0]
    owner = owner_ref[...]
    mine = iota((PEERS, rows), 0) == owner
    upto = ones_where(iota((rows, rows), 0) <= iota((rows, rows), 1))
    count = dot(ones_where(mine), upto)
    rank = jnp.sum(jnp.where(mine, count, 0.0), axis=0, keepdims=True).astype(jnp.int32) - 1
    pos = owner * CAP + rank
    pos_ref[...] = pos
    half = SLOTS // 2
    for part in range(2):
        place = ones_where(iota((half, rows), 0) + part * half == pos)
        sent = dot(place, rows_ref[...]).astype(BF)
        peers = pl.ds(part * (PEERS // 2), PEERS // 2)
        for c in range(COLS):
            pay_ref[peers, c * CAP : (c + 1) * CAP, :] = sent[:, c * LANES : (c + 1) * LANES].reshape(
                PEERS // 2, CAP, LANES
            )
    tags = jnp.where(mine, (list_ref[...] + 1).astype(F32), 0.0).astype(BF)
    at_rank = ones_where(iota((LANES, rows), 0) == rank)
    tag_rows = lax.dot_general(tags, at_rank, NT, preferred_element_type=F32)
    pay_ref[:, COLS * CAP :, :] = jnp.broadcast_to(
        tag_rows[:, None, :], (PEERS, PAY - COLS * CAP, LANES)
    ).astype(BF)


def pack(rows, owner, lists):
    return pl.pallas_call(
        pack_kernel,
        out_shape=(
            jax.ShapeDtypeStruct((PEERS, PAY, LANES), BF),
            jax.ShapeDtypeStruct(owner.shape, jnp.int32),
        ),
        in_specs=[VMEM] * 3,
        out_specs=(VMEM, VMEM),
        name="pack_rows",
        cost_estimate=pl.CostEstimate(flops=2**29, bytes_accessed=2**21, transcendentals=0),
    )(rows, owner, lists)


def pick_kernel(pos_ref, pick_ref):
    rows = pick_ref.shape[0]
    pos = pos_ref[...].astype(F32)
    column = jnp.sum(
        jnp.where(iota((rows, rows), 0) == iota((rows, rows), 1), pos, 0.0), axis=1, keepdims=True
    ).astype(jnp.int32)
    pick_ref[...] = ones_where(iota(pick_ref.shape, 1) == column)


def pick_matrix(pos):
    return pl.pallas_call(
        pick_kernel,
        out_shape=jax.ShapeDtypeStruct((pos.shape[1], SLOTS), BF),
        in_specs=[VMEM],
        out_specs=VMEM,
        name="pick_matrix",
        cost_estimate=pl.CostEstimate(flops=2**28, bytes_accessed=2**20, transcendentals=0),
    )(pos)


def unpick_kernel(pick_ref, back_ref, out_ref):
    out_ref[...] = dot(pick_ref[...], back_ref[...]).astype(BF)


def unpick(pick, back):
    return pl.pallas_call(
        unpick_kernel,
        out_shape=jax.ShapeDtypeStruct((pick.shape[0], D), BF),
        in_specs=[VMEM] * 2,
        out_specs=VMEM,
        name="unpick_rows",
        cost_estimate=pl.CostEstimate(flops=2**29, bytes_accessed=2**21, transcendentals=0),
    )(pick, back)


def main_kernel(
    y_ref,
    pay_ref,
    user_ref,
    cross_ref,
    up_ref,
    down_ref,
    near_ref,
    far_ref,
    out_w_ref,
    out_ref,
    mixed_ref,
    in_ref,
    even_q,
    odd_q,
    even_k,
    odd_k,
    values_ref,
):
    share = near_ref.shape[0] // 8
    y, core = y_ref[0], y_ref[1]
    for i, step in enumerate((1, 0, -1, -2, -3, -4, 3, 2)):
        chip = lax.rem(y + step + 8, 8) * 2
        for ref, which in ((near_ref, core), (far_ref, 1 - core)):
            spot = pl.multiple_of((chip + which) * share, share)
            in_ref[pl.ds(spot, share), :] = ref[i * share : (i + 1) * share, :]

    low = iota((BLOCK, LANES), 1) < LANES // 2
    lane = iota((BLOCK, LANES), 1)
    fit = lane == lax.rem(iota((BLOCK, LANES), 0), CAP)
    spread = ones_where(iota((LANES, LANES), 0) >= 0)
    head = D // HEADS
    mean = jnp.where(
        iota((BLOCK, BLOCK), 0) // head == iota((BLOCK, BLOCK), 1) // head, 1.0 / head, 0.0
    ).astype(BF)
    ones_low = ones_where(low)
    ones_high = ones_where(jnp.logical_not(low))

    def normed(block, scale):
        square = (block * block).astype(BF)
        parts = []
        for j in range(D // BLOCK):
            cut = slice(j * BLOCK, (j + 1) * BLOCK)
            parts.append(block[:, cut] * (lax.rsqrt(dot(square[:, cut], mean) + 1e-06) * scale))
        return jnp.concatenate(parts, axis=1)

    def prepare(b, carry):
        peers = pl.ds(b * (BLOCK // CAP), BLOCK // CAP)
        rows = pl.ds(pl.multiple_of(b * BLOCK, BLOCK), BLOCK)
        tag8 = pay_ref[peers, COLS * CAP :, :].astype(F32)
        tag32 = jnp.concatenate([tag8] * (CAP // 8), axis=1).reshape(BLOCK, LANES)
        tag = dot(jnp.where(fit, tag32, 0.0).astype(BF), spread)
        first, second = tag == 1.0, tag == 2.0
        combined = []
        for c in range(COLS):
            cut = slice(c * LANES, (c + 1) * LANES)
            x = pay_ref[peers, c * CAP : (c + 1) * CAP, :].reshape(BLOCK, LANES).astype(F32)
            user = jnp.where(second, user_ref[1:2, cut].astype(F32), user_ref[0:1, cut].astype(F32))
            combined.append((x + user).astype(BF))
        combined = jnp.concatenate(combined, axis=1)
        wide = combined.astype(F32)
        crossed = (wide * dot(combined, cross_ref[...]) + wide).astype(BF)
        active = jnp.maximum(dot(crossed, up_ref[...]), 0.0).astype(BF)
        mixed = (crossed.astype(F32) + dot(active, down_ref[...])).astype(BF)
        mixed_ref[rows, :] = mixed
        queries = normed(dot(mixed, in_ref[:, :D]), head**-0.5)
        keys = normed(dot(mixed, in_ref[:, D : 2 * D]), 1.0)
        values = dot(mixed, in_ref[:, 2 * D :]).astype(BF)

        odd_lane = lax.rem(lane, LANES // 2)
        query_mark = jnp.where(
            jnp.logical_or(
                jnp.logical_and(odd_lane == 0, first), jnp.logical_and(odd_lane == 1, second)
            ),
            -APART,
            0.0,
        )
        key_mark = jnp.where(
            jnp.logical_or(
                jnp.logical_and(odd_lane == 0, jnp.logical_not(first)),
                jnp.logical_and(odd_lane == 1, jnp.logical_not(second)),
            ),
            1.0,
            0.0,
        )
        for p in range(HEADS // 2):
            cut = slice(p * LANES, (p + 1) * LANES)
            even_q[rows, cut] = jnp.where(low, queries[:, cut], query_mark).astype(BF)
            odd_q[rows, cut] = jnp.where(low, query_mark, queries[:, cut]).astype(BF)
            even_k[rows, cut] = jnp.where(low, keys[:, cut], key_mark).astype(BF)
            odd_k[rows, cut] = jnp.where(low, key_mark, keys[:, cut]).astype(BF)
            value = values[:, cut].astype(F32)
            values_ref[p, rows, :LANES] = jnp.where(low, value, 0.0).astype(BF)
            values_ref[p, rows, LANES:] = ones_low
            later = pl.ds(pl.multiple_of(SLOTS + b * BLOCK, BLOCK), BLOCK)
            values_ref[p, later, :LANES] = jnp.where(low, 0.0, value).astype(BF)
            values_ref[p, later, LANES:] = ones_high
        return carry

    lax.fori_loop(0, SLOTS // BLOCK, prepare, 0)

    def attend(b, carry):
        rows = pl.ds(pl.multiple_of(b * BLOCK, BLOCK), BLOCK)
        attended = []
        for p in range(HEADS // 2):
            cut = slice(p * LANES, (p + 1) * LANES)
            powered = []
            for q, k in ((even_q, even_k), (odd_q, odd_k)):
                score = lax.dot_general(q[rows, cut], k[:, cut], NT, preferred_element_type=F32)
                powered.append(jnp.exp(score).astype(BF))
            summed = dot(powered[0], values_ref[p, :SLOTS, :]) + dot(
                powered[1], values_ref[p, SLOTS:, :]
            )
            attended.append((summed[:, :LANES] / summed[:, LANES:]).astype(BF))
        attended = jnp.concatenate(attended, axis=1)
        out_ref[rows, :] = (
            mixed_ref[rows, :].astype(F32) + dot(attended, out_w_ref[...])
        ).astype(BF)
        return carry

    lax.fori_loop(0, SLOTS // BLOCK, attend, 0)


def rerank(place, pay, users, cross, up, down, near, far, out_w):
    wide = pltpu.VMEM((SLOTS, D), BF)
    return pl.pallas_call(
        main_kernel,
        out_shape=jax.ShapeDtypeStruct((SLOTS, D), BF),
        in_specs=[pl.BlockSpec(memory_space=pltpu.SMEM)] + [VMEM] * 8,
        out_specs=VMEM,
        scratch_shapes=[
            wide,
            pltpu.VMEM((D, 3 * D), BF),
            wide,
            wide,
            wide,
            wide,
            pltpu.VMEM((HEADS // 2, 2 * SLOTS, 2 * LANES), BF),
        ],
        compiler_params=pltpu.CompilerParams(vmem_limit_bytes=48 * 2**20),
        name="rerank_lists",
        cost_estimate=pl.CostEstimate(flops=2**34, bytes_accessed=2**23, transcendentals=2**23),
    )(place, pay, users, cross, up, down, near, far, out_w)


def exchange(values):
    return lax.all_to_all(values, "cand", split_axis=0, concat_axis=0, tiled=True)


def along_y(steps):
    return [(i, (i + 2 * steps) % 16) for i in range(16)]


def gather_projection(part):
    share = part.shape[0]
    back = lax.ppermute(part, "req", along_y(1))
    ahead = lax.ppermute(part, "req", along_y(7))
    three = jnp.concatenate([ahead, part, back], axis=0)
    behind = lax.ppermute(three, "req", along_y(3))
    front = lax.ppermute(three[share:], "req", along_y(5))
    near = jnp.concatenate([three, behind, front], axis=0)
    far = lax.ppermute(near, "req", [(i, i ^ 1) for i in range(16)])
    return near, far


def local(
    cand_rows,
    user_rows,
    row_owner,
    row_list,
    cross_weight,
    up_weight,
    down_weight,
    project_in,
    project_out,
):
    pay, pos = pack(cand_rows[0], row_owner.reshape(1, -1), row_list)
    arrived = exchange(pay)
    near, far = gather_projection(project_in)
    pick = pick_matrix(pos)
    req = lax.axis_index("req")
    place = jnp.stack([req // 2, req % 2]).astype(jnp.int32)
    result = rerank(
        place, arrived, user_rows[0], cross_weight, up_weight, down_weight, near, far, project_out
    )
    back = exchange(result.reshape(PEERS, CAP, D))
    return unpick(pick, back.reshape(SLOTS, D))[None]


def solution(mesh):
    in_specs = (
        P("req", "cand", None),
        P("req", "cand", None),
        P("req", "cand", None),
        P("req", "cand"),
        P(),
        P(),
        P(),
        P("req", None),
        P(),
    )
    out_specs = P("req", "cand", None)
    return jax.shard_map(local, mesh=mesh, in_specs=in_specs, out_specs=out_specs, check_vma=False)
```

time: 229 us -> 126 us (0.55)
  the two profiles are of different devices: /device:TPU:24 before, /device:TPU:64 now
where the time goes in v1:
time: 126 us; the launch traced here: 125 us
  waiting for transfers between devices  49.8 us (40%)
  starting transfers between devices  39.5 us (31%)
  Pallas kernels  31 us (25%)
  local copies, waits for them, and re-layouts  4.51 us (4%)
    all_to_all x2, waiting for transfers between devices, exchange(): lax.all_to_all(values, 'cand', split_axis=0, concat_axis=0, tiled=True)  26.9 us
    pallas_call x1, Pallas kernels, rerank(): pl.pallas_call(main_kernel, out_shape=jax.ShapeDtypeStruct((SLOTS, D), BF...  23.1 us
    all_to_all x2, starting transfers between devices, exchange(): lax.all_to_all(values, 'cand', split_axis=0, concat_axis=0, tiled=True)  22.5 us
    ppermute x1, waiting for transfers between devices, gather_projection(): behind = lax.ppermute(three, 'req', along_y(3))  20.7 us
    ppermute x1, starting transfers between devices, gather_projection(): front = lax.ppermute(three[share:], 'req', along_y(5))  5.62 us
    unnamed x22, local copies, waits for them, and re-layouts  4.49 us
    ppermute x1, starting transfers between devices, gather_projection(): ahead = lax.ppermute(part, 'req', along_y(7))  3.82 us
    ppermute x1, starting transfers between devices, gather_projection(): back = lax.ppermute(part, 'req', along_y(1))  3.47 us
  transfers between devices with their start and end apart: 7, of which 3 were waited for; matrix products, arithmetic and copies ran while one was open for 2% of the time, Pallas kernels for 4%

profile of v1, /device:TPU:64, one launch (start us, length us, event | category | flops | bytes accessed | tf_op | source)
XLA Modules:
  0.0 125.2 jit_solution(13463161634728035582)
XLA Ops:
  0.0 3.5 %collective-permute-start.1 = (bf16[32,1536]{1,0:T(8,128)(2,1)}, bf16[32,1536]{1,0:T(8,128)(2,1)S(1)}, u32[]{:S(2)}, u32[]{:S(2)}) collective-permute-start(bf16[32,1536]{1,0:T(8,128)(2,1)} %param.16), channel_id=1, source_target_pairs={{0,64},{32,96},{64,128},{96,160},{128,192},{160,224},{192,256},{22... | collective-permute-start | bytes 294920 | tf_op jit(solution)/shard_map/ppermute | solution.py:266
  3.5 3.8 %collective-permute-start = (bf16[32,1536]{1,0:T(8,128)(2,1)}, bf16[32,1536]{1,0:T(8,128)(2,1)S(1)}, u32[]{:S(2)}, u32[]{:S(2)}) collective-permute-start(bf16[32,1536]{1,0:T(8,128)(2,1)} %param.16), channel_id=1, source_target_pairs={{0,448},{32,480},{64,0},{96,32},{128,64},{160,96},{192,128},{224,1... | collective-permute-start | bytes 294920 | tf_op jit(solution)/shard_map/ppermute | solution.py:267
  7.3 3.0 %pack_rows.1 = (bf16[32,136,128]{2,1,0:T(8,128)(2,1)}, s32[1,512]{1,0:T(1,128)}) custom-call(bf16[512,512]{1,0:T(8,128)(2,1)} %bitcast.10, s32[1,512]{1,0:T(1,128)} %bitcast.11, s32[1,512]{1,0:T(1,128)} %list_ref.1), custom_call_target="tpu_custom_call" | custom-call | flops 536870912 | bytes 2097152 | tf_op jit(solution)/shard_map/pack_rows/pallas_call | solution.py:63
  10.3 12.8 %all-to-all-start = ((bf16[32,136,128]{2,1,0:T(8,128)(2,1)}), bf16[32,136,128]{2,1,0:T(8,128)(2,1)}, u32[]{:S(2)}, u32[]{:S(2)}) async-start(bf16[32,136,128]{2,1,0:T(8,128)(2,1)} %get-tuple-element.8), calls=%async_computation | async-start | bytes 2228224 | tf_op jit(solution)/shard_map/all_to_all | solution.py:257
  23.1 0.0 collective-permute-done.1
  23.1 0.0 copy-done.6
  23.1 0.0 copy-start
  23.1 0.0 copy-start.1
  23.1 0.0 copy-start.4
  23.2 5.6 %collective-permute-start.3 = (bf16[64,1536]{1,0:T(8,128)(2,1)S(1)}, bf16[64,1536]{1,0:T(8,128)(2,1)S(1)}, u32[]{:S(2)}, u32[]{:S(2)}) collective-permute-start(bf16[64,1536]{1,0:T(8,128)(2,1)S(1)} %pad_maximum_fusion.1), channel_id=1, source_target_pairs={{0,320},{32,352},{64,384},{96,416},{128,448},{160,480},{192,0},{22... | collective-permute-start | bytes 589832 | tf_op jit(solution)/shard_map/ppermute | solution.py:270
  28.8 0.0 collective-permute-done
  28.8 0.0 copy-start.8
  28.8 0.0 copy-done.7
  28.9 0.6 copy-done.8
  29.4 2.1 %collective-permute-start.2 = (bf16[96,1536]{1,0:T(8,128)(2,1)S(1)}, bf16[96,1536]{1,0:T(8,128)(2,1)S(1)}, u32[]{:S(2)}, u32[]{:S(2)}) collective-permute-start(bf16[96,1536]{1,0:T(8,128)(2,1)S(1)} %pad_maximum_fusion), channel_id=1, source_target_pairs={{0,192},{32,224},{64,256},{96,288},{128,320},{160,352},{192,384},{... | collective-permute-start | bytes 884744 | tf_op jit(solution)/shard_map/ppermute | solution.py:269
  31.6 0.9 constant_dynamic-update-slice_fusion.4
  32.5 0.9 constant_dynamic-update-slice_fusion.2
  33.4 20.7 %collective-permute-done.2 = bf16[96,1536]{1,0:T(8,128)(2,1)S(1)} collective-permute-done((bf16[96,1536]{1,0:T(8,128)(2,1)S(1)}, bf16[96,1536]{1,0:T(8,128)(2,1)S(1)}, u32[]{:S(2)}, u32[]{:S(2)}) %collective-permute-start.2) | collective-permute-done | bytes 294944 | tf_op jit(solution)/shard_map/ppermute | solution.py:269
  54.1 0.0 collective-permute-done.3
  54.1 1.9 %collective-permute-start.4 = (bf16[256,1536]{1,0:T(8,128)(2,1)S(1)}, bf16[256,1536]{1,0:T(8,128)(2,1)}, u32[]{:S(2)}, u32[]{:S(2)}) collective-permute-start(bf16[256,1536]{1,0:T(8,128)(2,1)S(1)} %constant_dynamic-update-slice_fusion.near_ref), channel_id=1, source_target_pairs={{0,32},{32,0},{64,96},{96,64},{128,160},{160,128},{192,224},{224,1... | collective-permute-start | bytes 2359304 | tf_op jit(solution)/shard_map/ppermute | solution.py:272
  56.1 0.1 pad_add_fusion.y_ref
  56.2 2.3 %collective-permute-done.4.far_ref = bf16[256,1536]{1,0:T(8,128)(2,1)} collective-permute-done((bf16[256,1536]{1,0:T(8,128)(2,1)S(1)}, bf16[256,1536]{1,0:T(8,128)(2,1)}, u32[]{:S(2)}, u32[]{:S(2)}) %collective-permute-start.4) | collective-permute-done | bytes 786464 | tf_op jit(solution)/shard_map/ppermute | solution.py:272
  58.4 0.0 all-to-all-done.pay_ref
  58.4 0.0 copy-done.2
  58.5 0.0 copy-start.3
  58.5 1.0 copy-done.3
  59.5 23.1 %rerank_lists.1 = bf16[1024,512]{1,0:T(8,128)(2,1)} custom-call(s32[2]{0:T(128)S(1)} %pad_add_fusion.y_ref, bf16[32,136,128]{2,1,0:T(8,128)(2,1)} %all-to-all-done.pay_ref, bf16[2,512]{1,0:T(2,128)(2,1)S(1)} %bitcast.8, bf16[512,512]{1,0:T(8,128)(2,1)S(1)} %copy-done.2, bf16[512,1024]{1,0:T(8,128)(2,1)S(1)} %copy-done, bf16[1024,512]{1,0:T(8,128)(2,1)S(1)} %copy-done.1, ...), custom_call_target="tpu_custom_call" | custom-call | flops 17179869184 | bytes 8388608 | tf_op jit(solution)/shard_map/rerank_lists/pallas_call | solution.py:236
  82.6 9.8 %all-to-all-start.1 = ((bf16[32,32,512]{2,1,0:T(8,128)(2,1)}), bf16[32,32,512]{2,1,0:T(8,128)(2,1)S(1)}, u32[]{:S(2)}, u32[]{:S(2)}) async-start(bf16[32,32,512]{2,1,0:T(8,128)(2,1)} %bitcast.5), calls=%async_computation.1 | async-start | bytes 2097152 | tf_op jit(solution)/shard_map/all_to_all | solution.py:257
  92.4 1.9 %pick_matrix.1.pick_ref = bf16[512,1024]{1,0:T(8,128)(2,1)} custom-call(s32[1,512]{1,0:T(1,128)} %get-tuple-element.7.pos_ref), custom_call_target="tpu_custom_call" | custom-call | flops 268435456 | bytes 1048576 | tf_op jit(solution)/shard_map/pick_matrix/pallas_call | solution.py:86
  94.3 26.9 %all-to-all-done.1 = bf16[32,32,512]{2,1,0:T(8,128)(2,1)S(1)} async-done(((bf16[32,32,512]{2,1,0:T(8,128)(2,1)}), bf16[32,32,512]{2,1,0:T(8,128)(2,1)S(1)}, u32[]{:S(2)}, u32[]{:S(2)}) %all-to-all-start.1) | async-done | bytes 1048608 | tf_op jit(solution)/shard_map/all_to_all | solution.py:257
  121.2 1.0 copy-done.5
  122.2 3.0 %unpick_rows.1 = bf16[512,512]{1,0:T(8,128)(2,1)} custom-call(bf16[512,1024]{1,0:T(8,128)(2,1)} %pick_matrix.1.pick_ref, bf16[1024,512]{1,0:T(8,128)(2,1)} %bitcast.9), custom_call_target="tpu_custom_call" | custom-call | flops 536870912 | bytes 2097152 | tf_op jit(solution)/shard_map/unpick_rows/pallas_call | solution.py:101
  (12 shorter events, 0.1 us)
Async XLA Ops:
  0.0 23.1 %collective-permute-start.1 = (bf16[32,1536]{1,0:T(8,128)(2,1)}, bf16[32,1536]{1,0:T(8,128)(2,1)S(1)}, u32[]{:S(2)}, u32[]{:S(2)}) collective-permute-start(bf16[32,1536]{1,0:T(8,128)(2,1)} %param.16), channel_id=1, source_target_pairs={{0,64},{32,96},{64,128},{96,160},{128,192},{160,224},{192,256},{22... | collective-permute-start | bytes 294920 | tf_op jit(solution)/shard_map/ppermute | solution.py:266
  3.5 25.3 %collective-permute-start = (bf16[32,1536]{1,0:T(8,128)(2,1)}, bf16[32,1536]{1,0:T(8,128)(2,1)S(1)}, u32[]{:S(2)}, u32[]{:S(2)}) collective-permute-start(bf16[32,1536]{1,0:T(8,128)(2,1)} %param.16), channel_id=1, source_target_pairs={{0,448},{32,480},{64,0},{96,32},{128,64},{160,96},{192,128},{224,1... | collective-permute-start | bytes 294920 | tf_op jit(solution)/shard_map/ppermute | solution.py:267
  10.3 12.8 %copy-start.6 = (bf16[32,1536]{1,0:T(8,128)(2,1)S(1)}, bf16[32,1536]{1,0:T(8,128)(2,1)}, u32[]{:S(2)}) copy-start(bf16[32,1536]{1,0:T(8,128)(2,1)} %param.16) | copy-start | bytes 294916
  10.3 48.2 %copy-start.2 = (bf16[512,512]{1,0:T(8,128)(2,1)S(1)}, bf16[512,512]{1,0:T(8,128)(2,1)}, u32[]{:S(2)}) copy-start(bf16[512,512]{1,0:T(8,128)(2,1)} %cross_ref.1) | copy-start | bytes 1572868
  10.3 48.1 %all-to-all-start = ((bf16[32,136,128]{2,1,0:T(8,128)(2,1)}), bf16[32,136,128]{2,1,0:T(8,128)(2,1)}, u32[]{:S(2)}, u32[]{:S(2)}) async-start(bf16[32,136,128]{2,1,0:T(8,128)(2,1)} %get-tuple-element.8), calls=%async_computation | async-start | bytes 2228224 | tf_op jit(solution)/shard_map/all_to_all | solution.py:257
  23.1 5.8 %copy-start.7 = (bf16[32,1536]{1,0:T(8,128)(2,1)}, bf16[32,1536]{1,0:T(8,128)(2,1)S(1)}, u32[]{:S(2)}) copy-start(bf16[32,1536]{1,0:T(8,128)(2,1)S(1)} %collective-permute-done.1) | copy-start | bytes 294916
  23.1 35.3 %copy-start = (bf16[512,1024]{1,0:T(8,128)(2,1)S(1)}, bf16[512,1024]{1,0:T(8,128)(2,1)}, u32[]{:S(2)}) copy-start(bf16[512,1024]{1,0:T(8,128)(2,1)} %up_ref.1) | copy-start | bytes 3145732
  23.1 35.3 %copy-start.1 = (bf16[1024,512]{1,0:T(8,128)(2,1)S(1)}, bf16[1024,512]{1,0:T(8,128)(2,1)}, u32[]{:S(2)}) copy-start(bf16[1024,512]{1,0:T(8,128)(2,1)} %down_ref.1) | copy-start | bytes 3145732
  23.1 35.3 %copy-start.4 = (bf16[1,2,512]{2,1,0:T(2,128)(2,1)S(1)}, bf16[1,2,512]{2,1,0:T(2,128)(2,1)}, u32[]{:S(2)}) copy-start(bf16[1,2,512]{2,1,0:T(2,128)(2,1)} %param.10) | copy-start | bytes 6148
  23.2 30.9 %collective-permute-start.3 = (bf16[64,1536]{1,0:T(8,128)(2,1)S(1)}, bf16[64,1536]{1,0:T(8,128)(2,1)S(1)}, u32[]{:S(2)}, u32[]{:S(2)}) collective-permute-start(bf16[64,1536]{1,0:T(8,128)(2,1)S(1)} %pad_maximum_fusion.1), channel_id=1, source_target_pairs={{0,320},{32,352},{64,384},{96,416},{128,448},{160,480},{192,0},{22... | collective-permute-start | bytes 589832 | tf_op jit(solution)/shard_map/ppermute | solution.py:270
  28.8 0.6 copy-start.8
  29.4 24.6 %collective-permute-start.2 = (bf16[96,1536]{1,0:T(8,128)(2,1)S(1)}, bf16[96,1536]{1,0:T(8,128)(2,1)S(1)}, u32[]{:S(2)}, u32[]{:S(2)}) collective-permute-start(bf16[96,1536]{1,0:T(8,128)(2,1)S(1)} %pad_maximum_fusion), channel_id=1, source_target_pairs={{0,192},{32,224},{64,256},{96,288},{128,320},{160,352},{192,384},{... | collective-permute-start | bytes 884744 | tf_op jit(solution)/shard_map/ppermute | solution.py:269
  54.1 4.3 %collective-permute-start.4 = (bf16[256,1536]{1,0:T(8,128)(2,1)S(1)}, bf16[256,1536]{1,0:T(8,128)(2,1)}, u32[]{:S(2)}, u32[]{:S(2)}) collective-permute-start(bf16[256,1536]{1,0:T(8,128)(2,1)S(1)} %constant_dynamic-update-slice_fusion.near_ref), channel_id=1, source_target_pairs={{0,32},{32,0},{64,96},{96,64},{128,160},{160,128},{192,224},{224,1... | collective-permute-start | bytes 2359304 | tf_op jit(solution)/shard_map/ppermute | solution.py:272
  58.5 1.0 copy-start.3
  82.6 38.6 %all-to-all-start.1 = ((bf16[32,32,512]{2,1,0:T(8,128)(2,1)}), bf16[32,32,512]{2,1,0:T(8,128)(2,1)S(1)}, u32[]{:S(2)}, u32[]{:S(2)}) async-start(bf16[32,32,512]{2,1,0:T(8,128)(2,1)} %bitcast.5), calls=%async_computation.1 | async-start | bytes 2097152 | tf_op jit(solution)/shard_map/all_to_all | solution.py:257
  121.2 1.0 copy-start.5

commit v2 on v1

v2 whole, which is shorter than its diff:
```python
import jax
import jax.numpy as jnp
from jax import lax
from jax.experimental import pallas as pl
from jax.experimental.pallas import tpu as pltpu
from jax.sharding import PartitionSpec as P

HEADS = 8
PEERS = 32
CAP = 32
SLOTS = PEERS * CAP
D = 512
LANES = 128
COLS = D // LANES
PAY = COLS * CAP + 8
QBLOCK = 512
APART = 1024.0
BF = jnp.bfloat16
F32 = jnp.float32
VMEM = pl.BlockSpec(memory_space=pltpu.VMEM)
STEPS = (0, 4, 1, 5, 7, 3, 2, 6)
NT = (((1,), (1,)), ((), ()))


def iota(shape, dim):
    return lax.broadcasted_iota(jnp.int32, shape, dim)


def ones_where(cond):
    return jnp.where(cond, 1.0, 0.0).astype(BF)


def dot(a, b):
    return jnp.dot(a, b, preferred_element_type=F32)


def pack_kernel(rows_ref, owner_ref, list_ref, pay_ref, pos_ref):
    rows = rows_ref.shape[0]
    owner = owner_ref[...]
    mine = iota((PEERS, rows), 0) == owner
    upto = ones_where(iota((rows, rows), 0) <= iota((rows, rows), 1))
    count = dot(ones_where(mine), upto)
    rank = jnp.sum(jnp.where(mine, count, 0.0), axis=0, keepdims=True).astype(jnp.int32) - 1
    pos = owner * CAP + rank
    pos_ref[...] = pos
    half = SLOTS // 2
    for part in range(2):
        place = ones_where(iota((half, rows), 0) + part * half == pos)
        sent = dot(place, rows_ref[...]).astype(BF)
        peers = pl.ds(part * (PEERS // 2), PEERS // 2)
        for c in range(COLS):
            pay_ref[peers, c * CAP : (c + 1) * CAP, :] = sent[:, c * LANES : (c + 1) * LANES].reshape(
                PEERS // 2, CAP, LANES
            )
    tags = jnp.where(mine, (list_ref[...] + 1).astype(F32), 0.0).astype(BF)
    at_rank = ones_where(iota((LANES, rows), 0) == rank)
    tag_rows = lax.dot_general(tags, at_rank, NT, preferred_element_type=F32)
    pay_ref[:, COLS * CAP :, :] = jnp.broadcast_to(
        tag_rows[:, None, :], (PEERS, PAY - COLS * CAP, LANES)
    ).astype(BF)


def pack(rows, owner, lists):
    return pl.pallas_call(
        pack_kernel,
        out_shape=(
            jax.ShapeDtypeStruct((PEERS, PAY, LANES), BF),
            jax.ShapeDtypeStruct(owner.shape, jnp.int32),
        ),
        in_specs=[VMEM] * 3,
        out_specs=(VMEM, VMEM),
        name="pack_rows",
        cost_estimate=pl.CostEstimate(flops=2**29, bytes_accessed=2**21, transcendentals=0),
    )(rows, owner, lists)


def pick_kernel(pos_ref, pick_ref):
    rows = pick_ref.shape[0]
    pos = pos_ref[...].astype(F32)
    column = jnp.sum(
        jnp.where(iota((rows, rows), 0) == iota((rows, rows), 1), pos, 0.0), axis=1, keepdims=True
    ).astype(jnp.int32)
    pick_ref[...] = ones_where(iota(pick_ref.shape, 1) == column)


def pick_matrix(pos):
    return pl.pallas_call(
        pick_kernel,
        out_shape=jax.ShapeDtypeStruct((pos.shape[1], SLOTS), BF),
        in_specs=[VMEM],
        out_specs=VMEM,
        name="pick_matrix",
        cost_estimate=pl.CostEstimate(flops=2**36, bytes_accessed=2**28, transcendentals=0),
    )(pos)


def main_kernel(
    y_ref,
    pay_ref,
    user_ref,
    cross_ref,
    up_ref,
    down_ref,
    *refs,
):
    part_refs, (out_w_ref, out_ref) = refs[:8], refs[8:10]
    mixed_ref, in_ref, in_t, even_k, odd_k, queries_ref, values_ref, attended_ref = refs[10:]
    share = part_refs[0].shape[0] // 2
    y, core = y_ref[0], y_ref[1]
    for i, step in enumerate(STEPS):
        chip = lax.rem(y + step, 8) * 2
        for ref, which in ((part_refs[i // 2], core), (part_refs[4 + i // 2], 1 - core)):
            spot = pl.multiple_of((chip + which) * share, share)
            in_ref[pl.ds(spot, share), :] = ref[i % 2 * share : (i % 2 + 1) * share, :]

    in_t[...] = jnp.concatenate([in_ref[:, :D].T, in_ref[:, 2 * D :].T], axis=0)

    head = D // HEADS
    lane = iota((SLOTS, LANES), 1)
    low = lane < head
    fit = lane == lax.rem(iota((SLOTS, LANES), 0), CAP)
    spread = ones_where(iota((LANES, LANES), 0) >= 0)
    mean = jnp.where(
        iota((256, 256), 0) // head == iota((256, 256), 1) // head, 1.0 / head, 0.0
    ).astype(BF)

    tag8 = pay_ref[:, COLS * CAP :, :].astype(F32)
    tag32 = jnp.concatenate([tag8] * (CAP // 8), axis=1).reshape(SLOTS, LANES)
    tag_bf = jnp.where(fit, tag32, 0.0).astype(BF)
    tag = dot(tag_bf, spread)
    tag_t = lax.dot_general(spread[:head], tag_bf, NT, preferred_element_type=F32)
    first, second = tag == 1.0, tag == 2.0
    combined = []
    for c in range(COLS):
        cut = slice(c * LANES, (c + 1) * LANES)
        x = pay_ref[:, c * CAP : (c + 1) * CAP, :].reshape(SLOTS, LANES).astype(F32)
        user = jnp.where(second, user_ref[1:2, cut].astype(F32), user_ref[0:1, cut].astype(F32))
        combined.append((x + user).astype(BF))
    combined = jnp.concatenate(combined, axis=1)
    wide = combined.astype(F32)
    crossed = (wide * dot(combined, cross_ref[...]) + wide).astype(BF)
    active = jnp.maximum(dot(crossed, up_ref[...]), 0.0).astype(BF)
    mixed = (crossed.astype(F32) + dot(active, down_ref[...])).astype(BF)
    mixed_ref[...] = mixed

    keys = dot(mixed, in_ref[:, D : 2 * D])
    square = (keys * keys).astype(BF)
    spot = lax.rem(lane, head)
    key_mark = jnp.where(
        jnp.logical_or(
            jnp.logical_and(spot == 0, jnp.logical_not(first)),
            jnp.logical_and(spot == 1, jnp.logical_not(second)),
        ),
        1.0,
        0.0,
    )
    for j in range(D // 256):
        cut = slice(j * 256, (j + 1) * 256)
        normed = keys[:, cut] * lax.rsqrt(dot(square[:, cut], mean) + 1e-06)
        for i in range(2):
            key = normed[:, i * LANES : (i + 1) * LANES]
            even_k[2 * j + i, :, :] = jnp.where(low, key, key_mark).astype(BF)
            odd_k[2 * j + i, :, :] = jnp.where(low, key_mark, key).astype(BF)

    turned = lax.dot_general(in_t[...], mixed, NT, preferred_element_type=F32)
    row = iota((head, SLOTS), 0)
    query_mark = jnp.where(
        jnp.logical_or(
            jnp.logical_and(row == 0, tag_t == 1.0), jnp.logical_and(row == 1, tag_t == 2.0)
        ),
        -APART,
        0.0,
    ).astype(BF)
    for h in range(HEADS):
        query = turned[h * head : (h + 1) * head, :]
        level = jnp.mean(query * query, axis=0, keepdims=True)
        query = (query * (lax.rsqrt(level + 1e-06) * head**-0.5)).astype(BF)
        at = h % 2 * head
        queries_ref[h, at : at + head, :] = query
        queries_ref[h, head - at : 2 * head - at, :] = query_mark
        values_ref[h, :head, :] = turned[D + h * head : D + (h + 1) * head, :].astype(BF)
        values_ref[h, head:, :] = ones_where(iota((16, SLOTS), 0) >= 0)

    for p in range(HEADS // 2):
        pair = []
        for i, k in enumerate((even_k, odd_k)):
            h = 2 * p + i
            halves = []
            for j in range(SLOTS // QBLOCK):
                cut = slice(j * QBLOCK, (j + 1) * QBLOCK)
                powered = jnp.exp(dot(k[p], queries_ref[h, :, cut])).astype(BF)
                summed = dot(values_ref[h], powered)
                halves.append((summed[:head] / summed[head : head + 1]).astype(BF))
            pair.append(jnp.concatenate(halves, axis=1))
        attended_ref[p] = jnp.concatenate(pair, axis=0).T

    attended = jnp.concatenate([attended_ref[p] for p in range(HEADS // 2)], axis=1)
    out_ref[...] = (mixed_ref[...].astype(F32) + dot(attended, out_w_ref[...])).astype(BF)


def rerank(place, pay, users, cross, up, down, parts, out_w):
    wide = pltpu.VMEM((SLOTS, D), BF)
    pairs = pltpu.VMEM((HEADS // 2, SLOTS, LANES), BF)
    return pl.pallas_call(
        main_kernel,
        out_shape=jax.ShapeDtypeStruct((SLOTS, D), BF),
        in_specs=[pl.BlockSpec(memory_space=pltpu.SMEM)] + [VMEM] * (6 + len(parts)),
        out_specs=VMEM,
        scratch_shapes=[
            wide,
            pltpu.VMEM((D, 3 * D), BF),
            pltpu.VMEM((2 * D, D), BF),
            pairs,
            pairs,
            pltpu.VMEM((HEADS, LANES, SLOTS), BF),
            pltpu.VMEM((HEADS, D // HEADS + 16, SLOTS), BF),
            pairs,
        ],
        compiler_params=pltpu.CompilerParams(vmem_limit_bytes=48 * 2**20),
        name="rerank_lists",
        cost_estimate=pl.CostEstimate(flops=2**34, bytes_accessed=2**23, transcendentals=2**23),
    )(place, pay, users, cross, up, down, *parts, out_w)


def exchange(values):
    return lax.all_to_all(values, "cand", split_axis=0, concat_axis=0, tiled=True)


def along_y(steps):
    return [(i, (i + 2 * steps) % 16) for i in range(16)]


CORE = [(i, i ^ 1) for i in range(16)]


def gather_projection(part, opposite):
    pair = jnp.concatenate([part, opposite], axis=0)
    two = lax.ppermute(pair, "req", along_y(6))
    one = lax.ppermute(pair, "req", along_y(7))
    seven = lax.ppermute(pair, "req", along_y(1))
    near = (pair, one, seven, two)
    return near + tuple(lax.ppermute(piece, "req", CORE) for piece in near)


def local(
    cand_rows,
    user_rows,
    row_owner,
    row_list,
    cross_weight,
    up_weight,
    down_weight,
    project_in,
    project_out,
):
    opposite = lax.ppermute(project_in, "req", along_y(4))
    pay, pos = pack(cand_rows[0], row_owner.reshape(1, -1), row_list)
    arrived = exchange(pay)
    pick, opposite = lax.optimization_barrier((pick_matrix(pos), opposite))
    parts = gather_projection(project_in, opposite)
    req = lax.axis_index("req")
    place = jnp.stack([req // 2, req % 2]).astype(jnp.int32)
    result = rerank(
        place, arrived, user_rows[0], cross_weight, up_weight, down_weight, parts, project_out
    )
    back = exchange(result.reshape(PEERS, CAP, D))
    return dot(pick, back.reshape(SLOTS, D)).astype(BF)[None]


def solution(mesh):
    in_specs = (
        P("req", "cand", None),
        P("req", "cand", None),
        P("req", "cand", None),
        P("req", "cand"),
        P(),
        P(),
        P(),
        P("req", None),
        P(),
    )
    out_specs = P("req", "cand", None)
    return jax.shard_map(local, mesh=mesh, in_specs=in_specs, out_specs=out_specs, check_vma=False)
```

time: 126 us -> 103 us (0.82)
  waiting for transfers between devices: 49.8 us -> 9.79 us
  blocking collectives: 0 us -> 33.2 us
  Pallas kernels: 31 us -> 20.2 us
  local copies, waits for them, and re-layouts: 4.51 us -> 0.06 us
  starting transfers between devices: 39.5 us -> 37.8 us
  matrix products: 0 us -> 1.5 us
    all_to_all x0 -> x1, blocking collectives: none -> 33.2 us  [exchange(): lax.all_to_all(values, 'cand', split_axis=0, concat_axis=0, tiled=True)]
    all_to_all x2 -> x1, waiting for transfers between devices: 26.9 us -> 6.1 us  [exchange(): lax.all_to_all(values, 'cand', split_axis=0, concat_axis=0, tiled=True)]
    ppermute x5 -> x8, waiting for transfers between devices: 23 us -> 3.69 us  [the longest x1 2.04 us: gather_projection(): two = lax.ppermute(pair, 'req', along_y(6))]
    all_to_all x2 -> x1, starting transfers between devices: 22.5 us -> 12.6 us  [exchange(): lax.all_to_all(values, 'cand', split_axis=0, concat_axis=0, tiled=True)]
    ppermute x5 -> x8, starting transfers between devices: 17 us -> 25.2 us  [the longest x4 8.16 us: gather_projection(): return near + tuple((lax.ppermute(piece, 'req', CORE) for piece in near))]
    pallas_call x1, Pallas kernels: 23.1 us -> 15.1 us  [rerank(): pl.pallas_call(main_kernel, out_shape=jax.ShapeDtypeStruct((SLOTS, D), BF...]
    unnamed x22 -> x15, local copies, waits for them, and re-layouts: 4.49 us -> 0.05 us
    pallas_call x1 -> x0, Pallas kernels: 3.04 us -> none  [unpick(): pl.pallas_call(unpick_kernel, out_shape=jax.ShapeDtypeStruct((pick.shape[...]
  transfers between devices with their start and end apart: 7 -> 9, of which waited for: 3 -> 3; matrix products, arithmetic and copies ran while one was open for 2% -> 0% of each run, Pallas kernels for 4% -> 5%
where the time goes in v2:
time: 103 us
  starting transfers between devices  37.8 us (37%)
  blocking collectives  33.2 us (32%)
  Pallas kernels  20.2 us (20%)
  waiting for transfers between devices  9.79 us (10%)
  matrix products  1.5 us (1%)
    all_to_all x1, blocking collectives, exchange(): lax.all_to_all(values, 'cand', split_axis=0, concat_axis=0, tiled=True)  33.2 us
    pallas_call x1, Pallas kernels, rerank(): pl.pallas_call(main_kernel, out_shape=jax.ShapeDtypeStruct((SLOTS, D), BF...  15.1 us
    all_to_all x1, starting transfers between devices, exchange(): lax.all_to_all(values, 'cand', split_axis=0, concat_axis=0, tiled=True)  12.6 us
    ppermute x4, starting transfers between devices, gather_projection(): return near + tuple((lax.ppermute(piece, 'req', CORE) for piece in near))  8.16 us
    ppermute x1, starting transfers between devices, local(): opposite = lax.ppermute(project_in, 'req', along_y(4))  7.72 us
    all_to_all x1, waiting for transfers between devices, exchange(): lax.all_to_all(values, 'cand', split_axis=0, concat_axis=0, tiled=True)  6.1 us
    ppermute x1, starting transfers between devices, gather_projection(): one = lax.ppermute(pair, 'req', along_y(7))  3.57 us
    ppermute x1, starting transfers between devices, gather_projection(): seven = lax.ppermute(pair, 'req', along_y(1))  3.48 us
  transfers between devices with their start and end apart: 9, of which 3 were waited for; matrix products, arithmetic and copies ran while one was open for 0% of the time, Pallas kernels for 5%

profile of v2, /device:TPU:64, one launch (start us, length us, event | category | flops | bytes accessed | tf_op | source)
XLA Modules:
  0.0 102.9 jit_solution(7643231344979502097)
XLA Ops:
  0.0 7.7 %collective-permute-start = (bf16[32,1536]{1,0:T(8,128)(2,1)}, bf16[32,1536]{1,0:T(8,128)(2,1)S(1)}, u32[]{:S(2)}, u32[]{:S(2)}) collective-permute-start(bf16[32,1536]{1,0:T(8,128)(2,1)} %param.16), channel_id=1, source_target_pairs={{0,256},{32,288},{64,320},{96,352},{128,384},{160,416},{192,448},{... | collective-permute-start | bytes 294920 | tf_op jit(solution)/shard_map/ppermute | solution.py:256
  7.7 3.0 %pack_rows.1 = (bf16[32,136,128]{2,1,0:T(8,128)(2,1)}, s32[1,512]{1,0:T(1,128)}) custom-call(bf16[512,512]{1,0:T(8,128)(2,1)} %bitcast.14, s32[1,512]{1,0:T(1,128)} %bitcast.15, s32[1,512]{1,0:T(1,128)} %list_ref.1), custom_call_target="tpu_custom_call" | custom-call | flops 536870912 | bytes 2097152 | tf_op jit(solution)/shard_map/pack_rows/pallas_call | solution.py:64
  10.7 12.6 %all-to-all-start = ((bf16[32,136,128]{2,1,0:T(8,128)(2,1)}), bf16[32,136,128]{2,1,0:T(8,128)(2,1)}, u32[]{:S(2)}, u32[]{:S(2)}) async-start(bf16[32,136,128]{2,1,0:T(8,128)(2,1)} %get-tuple-element.11), calls=%async_computation | async-start | bytes 2228224 | tf_op jit(solution)/shard_map/all_to_all | solution.py:226
  23.4 0.0 copy-start.5
  23.4 0.0 copy-start
  23.4 0.0 copy-start.1
  23.4 0.0 copy-start.2
  23.4 0.0 copy-start.3
  23.4 0.0 copy-start.4
  23.4 2.1 %pick_matrix.1 = bf16[512,1024]{1,0:T(8,128)(2,1)} custom-call(s32[1,512]{1,0:T(1,128)} %get-tuple-element.9.pos_ref), custom_call_target="tpu_custom_call" | custom-call | flops 68719476736 | bytes 268435456 | tf_op jit(solution)/shard_map/pick_matrix/pallas_call | solution.py:87
  25.6 0.0 copy-done.5
  25.6 0.0 collective-permute-done
  25.6 2.2 %collective-permute-start.3 = (bf16[64,1536]{1,0:T(8,128)(2,1)S(1)}, bf16[64,1536]{1,0:T(8,128)(2,1)S(1)}, u32[]{:S(2)}, u32[]{:S(2)}) collective-permute-start(bf16[64,1536]{1,0:T(8,128)(2,1)S(1)} %constant_dynamic-update-slice_fusion.refs_0_), channel_id=1, source_target_pairs={{0,384},{32,416},{64,448},{96,480},{128,0},{160,32},{192,64},{224,... | collective-permute-start | bytes 589832 | tf_op jit(solution)/shard_map/ppermute | solution.py:238
  27.8 3.5 %collective-permute-start.2 = (bf16[64,1536]{1,0:T(8,128)(2,1)S(1)}, bf16[64,1536]{1,0:T(8,128)(2,1)}, u32[]{:S(2)}, u32[]{:S(2)}) collective-permute-start(bf16[64,1536]{1,0:T(8,128)(2,1)S(1)} %constant_dynamic-update-slice_fusion.refs_0_), channel_id=1, source_target_pairs={{0,64},{32,96},{64,128},{96,160},{128,192},{160,224},{192,256},{22... | collective-permute-start | bytes 589832 | tf_op jit(solution)/shard_map/ppermute | solution.py:240
  31.3 3.6 %collective-permute-start.1 = (bf16[64,1536]{1,0:T(8,128)(2,1)S(1)}, bf16[64,1536]{1,0:T(8,128)(2,1)}, u32[]{:S(2)}, u32[]{:S(2)}) collective-permute-start(bf16[64,1536]{1,0:T(8,128)(2,1)S(1)} %constant_dynamic-update-slice_fusion.refs_0_), channel_id=1, source_target_pairs={{0,448},{32,480},{64,0},{96,32},{128,64},{160,96},{192,128},{224,1... | collective-permute-start | bytes 589832 | tf_op jit(solution)/shard_map/ppermute | solution.py:239
  34.9 1.9 %collective-permute-start.4 = (bf16[64,1536]{1,0:T(8,128)(2,1)S(1)}, bf16[64,1536]{1,0:T(8,128)(2,1)}, u32[]{:S(2)}, u32[]{:S(2)}) collective-permute-start(bf16[64,1536]{1,0:T(8,128)(2,1)S(1)} %constant_dynamic-update-slice_fusion.refs_0_), channel_id=1, source_target_pairs={{0,32},{32,0},{64,96},{96,64},{128,160},{160,128},{192,224},{224,1... | collective-permute-start | bytes 589832 | tf_op jit(solution)/shard_map/ppermute | solution.py:242
  36.8 2.0 %collective-permute-done.3.refs_3_ = bf16[64,1536]{1,0:T(8,128)(2,1)S(1)} collective-permute-done((bf16[64,1536]{1,0:T(8,128)(2,1)S(1)}, bf16[64,1536]{1,0:T(8,128)(2,1)S(1)}, u32[]{:S(2)}, u32[]{:S(2)}) %collective-permute-start.3) | collective-permute-done | bytes 196640 | tf_op jit(solution)/shard_map/ppermute | solution.py:238
  38.9 1.9 %collective-permute-start.7 = (bf16[64,1536]{1,0:T(8,128)(2,1)S(1)}, bf16[64,1536]{1,0:T(8,128)(2,1)}, u32[]{:S(2)}, u32[]{:S(2)}) collective-permute-start(bf16[64,1536]{1,0:T(8,128)(2,1)S(1)} %collective-permute-done.3.refs_3_), channel_id=1, source_target_pairs={{0,32},{32,0},{64,96},{96,64},{128,160},{160,128},{192,224},{224,1... | collective-permute-start | bytes 589832 | tf_op jit(solution)/shard_map/ppermute | solution.py:242
  40.8 0.0 collective-permute-done.2.refs_2_
  40.8 2.4 %collective-permute-start.6 = (bf16[64,1536]{1,0:T(8,128)(2,1)}, bf16[64,1536]{1,0:T(8,128)(2,1)}, u32[]{:S(2)}, u32[]{:S(2)}) collective-permute-start(bf16[64,1536]{1,0:T(8,128)(2,1)} %collective-permute-done.2.refs_2_), channel_id=1, source_target_pairs={{0,32},{32,0},{64,96},{96,64},{128,160},{160,128},{192,224},{224,1... | collective-permute-start | bytes 589832 | tf_op jit(solution)/shard_map/ppermute | solution.py:242
  43.2 0.0 collective-permute-done.1.refs_1_
  43.2 1.9 %collective-permute-start.5 = (bf16[64,1536]{1,0:T(8,128)(2,1)}, bf16[64,1536]{1,0:T(8,128)(2,1)}, u32[]{:S(2)}, u32[]{:S(2)}) collective-permute-start(bf16[64,1536]{1,0:T(8,128)(2,1)} %collective-permute-done.1.refs_1_), channel_id=1, source_target_pairs={{0,32},{32,0},{64,96},{96,64},{128,160},{160,128},{192,224},{224,1... | collective-permute-start | bytes 589832 | tf_op jit(solution)/shard_map/ppermute | solution.py:242
  45.2 0.1 pad_add_fusion.y_ref
  45.3 0.0 collective-permute-done.4.refs_4_
  45.3 0.0 collective-permute-done.7.refs_7_
  45.3 0.0 collective-permute-done.6.refs_6_
  45.3 1.6 %collective-permute-done.5.refs_5_ = bf16[64,1536]{1,0:T(8,128)(2,1)} collective-permute-done((bf16[64,1536]{1,0:T(8,128)(2,1)}, bf16[64,1536]{1,0:T(8,128)(2,1)}, u32[]{:S(2)}, u32[]{:S(2)}) %collective-permute-start.5) | collective-permute-done | bytes 196640 | tf_op jit(solution)/shard_map/ppermute | solution.py:242
  46.9 6.1 %all-to-all-done.pay_ref = bf16[32,136,128]{2,1,0:T(8,128)(2,1)} async-done(((bf16[32,136,128]{2,1,0:T(8,128)(2,1)}), bf16[32,136,128]{2,1,0:T(8,128)(2,1)}, u32[]{:S(2)}, u32[]{:S(2)}) %all-to-all-start) | async-done | bytes 1114144 | tf_op jit(solution)/shard_map/all_to_all | solution.py:226
  53.0 0.0 copy-done.1
  53.0 15.1 %rerank_lists.1 = bf16[1024,512]{1,0:T(8,128)(2,1)S(1)} custom-call(s32[2]{0:T(128)S(1)} %pad_add_fusion.y_ref, bf16[32,136,128]{2,1,0:T(8,128)(2,1)} %all-to-all-done.pay_ref, bf16[2,512]{1,0:T(2,128)(2,1)S(1)} %bitcast.12, bf16[512,512]{1,0:T(8,128)(2,1)S(1)} %copy-done.2, bf16[512,1024]{1,0:T(8,128)(2,1)S(1)} %copy-done, bf16[1024,512]{1,0:T(8,128)(2,1)S(1)} %copy-done.1, ...), custom_call_target="tpu_custom_call" | custom-call | flops 17179869184 | bytes 8388608 | tf_op jit(solution)/shard_map/rerank_lists/pallas_call | solution.py:204
  68.2 33.2 %all_to_all.10 = bf16[32,32,512]{2,1,0:T(8,128)(2,1)S(1)} all-to-all(bf16[32,32,512]{2,1,0:T(8,128)(2,1)S(1)} %bitcast.11), channel_id=1, replica_groups=mesh['req'=16,'cand'=32] {'cand'}, dimensions={0} | all-to-all | bytes 2097152 | tf_op jit(solution)/shard_map/all_to_all | solution.py:226
  101.4 1.5 %fusion = bf16[1,512,512]{2,1,0:T(8,128)(2,1)} fusion(bf16[512,1024]{1,0:T(8,128)(2,1)S(1)} %copy-done.6, bf16[1024,512]{1,0:T(8,128)(2,1)S(1)} %bitcast.13), kind=kOutput, calls=%fused_computation.1 | convolution fusion | flops 537133056 | bytes 2621440 | tf_op jit(solution)/shard_map/dot_general | solution.py:34
  (8 shorter events, 0.0 us)
Async XLA Ops:
  0.0 25.6 %collective-permute-start = (bf16[32,1536]{1,0:T(8,128)(2,1)}, bf16[32,1536]{1,0:T(8,128)(2,1)S(1)}, u32[]{:S(2)}, u32[]{:S(2)}) collective-permute-start(bf16[32,1536]{1,0:T(8,128)(2,1)} %param.16), channel_id=1, source_target_pairs={{0,256},{32,288},{64,320},{96,352},{128,384},{160,416},{192,448},{... | collective-permute-start | bytes 294920 | tf_op jit(solution)/shard_map/ppermute | solution.py:256
  10.7 42.3 %all-to-all-start = ((bf16[32,136,128]{2,1,0:T(8,128)(2,1)}), bf16[32,136,128]{2,1,0:T(8,128)(2,1)}, u32[]{:S(2)}, u32[]{:S(2)}) async-start(bf16[32,136,128]{2,1,0:T(8,128)(2,1)} %get-tuple-element.11), calls=%async_computation | async-start | bytes 2228224 | tf_op jit(solution)/shard_map/all_to_all | solution.py:226
  23.4 2.2 %copy-start.5 = (bf16[32,1536]{1,0:T(8,128)(2,1)S(1)}, bf16[32,1536]{1,0:T(8,128)(2,1)}, u32[]{:S(2)}) copy-start(bf16[32,1536]{1,0:T(8,128)(2,1)} %param.16) | copy-start | bytes 294916
  23.4 29.6 %copy-start = (bf16[512,1024]{1,0:T(8,128)(2,1)S(1)}, bf16[512,1024]{1,0:T(8,128)(2,1)}, u32[]{:S(2)}) copy-start(bf16[512,1024]{1,0:T(8,128)(2,1)} %up_ref.1) | copy-start | bytes 3145732
  23.4 29.6 %copy-start.1 = (bf16[1024,512]{1,0:T(8,128)(2,1)S(1)}, bf16[1024,512]{1,0:T(8,128)(2,1)}, u32[]{:S(2)}) copy-start(bf16[1024,512]{1,0:T(8,128)(2,1)} %down_ref.1) | copy-start | bytes 3145732
  23.4 29.6 %copy-start.2 = (bf16[512,512]{1,0:T(8,128)(2,1)S(1)}, bf16[512,512]{1,0:T(8,128)(2,1)}, u32[]{:S(2)}) copy-start(bf16[512,512]{1,0:T(8,128)(2,1)} %cross_ref.1) | copy-start | bytes 1572868
  23.4 29.6 %copy-start.3 = (bf16[512,512]{1,0:T(8,128)(2,1)S(1)}, bf16[512,512]{1,0:T(8,128)(2,1)}, u32[]{:S(2)}) copy-start(bf16[512,512]{1,0:T(8,128)(2,1)} %refs_8_.1) | copy-start | bytes 1572868
  23.4 29.6 %copy-start.4 = (bf16[1,2,512]{2,1,0:T(2,128)(2,1)S(1)}, bf16[1,2,512]{2,1,0:T(2,128)(2,1)}, u32[]{:S(2)}) copy-start(bf16[1,2,512]{2,1,0:T(2,128)(2,1)} %param.10) | copy-start | bytes 6148
  25.6 13.3 %collective-permute-start.3 = (bf16[64,1536]{1,0:T(8,128)(2,1)S(1)}, bf16[64,1536]{1,0:T(8,128)(2,1)S(1)}, u32[]{:S(2)}, u32[]{:S(2)}) collective-permute-start(bf16[64,1536]{1,0:T(8,128)(2,1)S(1)} %constant_dynamic-update-slice_fusion.refs_0_), channel_id=1, source_target_pairs={{0,384},{32,416},{64,448},{96,480},{128,0},{160,32},{192,64},{224,... | collective-permute-start | bytes 589832 | tf_op jit(solution)/shard_map/ppermute | solution.py:238
  27.8 13.0 %collective-permute-start.2 = (bf16[64,1536]{1,0:T(8,128)(2,1)S(1)}, bf16[64,1536]{1,0:T(8,128)(2,1)}, u32[]{:S(2)}, u32[]{:S(2)}) collective-permute-start(bf16[64,1536]{1,0:T(8,128)(2,1)S(1)} %constant_dynamic-update-slice_fusion.refs_0_), channel_id=1, source_target_pairs={{0,64},{32,96},{64,128},{96,160},{128,192},{160,224},{192,256},{22... | collective-permute-start | bytes 589832 | tf_op jit(solution)/shard_map/ppermute | solution.py:240
  31.3 11.9 %collective-permute-start.1 = (bf16[64,1536]{1,0:T(8,128)(2,1)S(1)}, bf16[64,1536]{1,0:T(8,128)(2,1)}, u32[]{:S(2)}, u32[]{:S(2)}) collective-permute-start(bf16[64,1536]{1,0:T(8,128)(2,1)S(1)} %constant_dynamic-update-slice_fusion.refs_0_), channel_id=1, source_target_pairs={{0,448},{32,480},{64,0},{96,32},{128,64},{160,96},{192,128},{224,1... | collective-permute-start | bytes 589832 | tf_op jit(solution)/shard_map/ppermute | solution.py:239
  34.9 10.3 %collective-permute-start.4 = (bf16[64,1536]{1,0:T(8,128)(2,1)S(1)}, bf16[64,1536]{1,0:T(8,128)(2,1)}, u32[]{:S(2)}, u32[]{:S(2)}) collective-permute-start(bf16[64,1536]{1,0:T(8,128)(2,1)S(1)} %constant_dynamic-update-slice_fusion.refs_0_), channel_id=1, source_target_pairs={{0,32},{32,0},{64,96},{96,64},{128,160},{160,128},{192,224},{224,1... | collective-permute-start | bytes 589832 | tf_op jit(solution)/shard_map/ppermute | solution.py:242
  38.9 6.4 %collective-permute-start.7 = (bf16[64,1536]{1,0:T(8,128)(2,1)S(1)}, bf16[64,1536]{1,0:T(8,128)(2,1)}, u32[]{:S(2)}, u32[]{:S(2)}) collective-permute-start(bf16[64,1536]{1,0:T(8,128)(2,1)S(1)} %collective-permute-done.3.refs_3_), channel_id=1, source_target_pairs={{0,32},{32,0},{64,96},{96,64},{128,160},{160,128},{192,224},{224,1... | collective-permute-start | bytes 589832 | tf_op jit(solution)/shard_map/ppermute | solution.py:242
  40.8 4.5 %collective-permute-start.6 = (bf16[64,1536]{1,0:T(8,128)(2,1)}, bf16[64,1536]{1,0:T(8,128)(2,1)}, u32[]{:S(2)}, u32[]{:S(2)}) collective-permute-start(bf16[64,1536]{1,0:T(8,128)(2,1)} %collective-permute-done.2.refs_2_), channel_id=1, source_target_pairs={{0,32},{32,0},{64,96},{96,64},{128,160},{160,128},{192,224},{224,1... | collective-permute-start | bytes 589832 | tf_op jit(solution)/shard_map/ppermute | solution.py:242
  43.2 3.7 %collective-permute-start.5 = (bf16[64,1536]{1,0:T(8,128)(2,1)}, bf16[64,1536]{1,0:T(8,128)(2,1)}, u32[]{:S(2)}, u32[]{:S(2)}) collective-permute-start(bf16[64,1536]{1,0:T(8,128)(2,1)} %collective-permute-done.1.refs_1_), channel_id=1, source_target_pairs={{0,32},{32,0},{64,96},{96,64},{128,160},{160,128},{192,224},{224,1... | collective-permute-start | bytes 589832 | tf_op jit(solution)/shard_map/ppermute | solution.py:242
  68.1 33.2 %copy-start.6 = (bf16[512,1024]{1,0:T(8,128)(2,1)S(1)}, bf16[512,1024]{1,0:T(8,128)(2,1)}, u32[]{:S(2)}) copy-start(bf16[512,1024]{1,0:T(8,128)(2,1)} %pick_matrix.1) | copy-start | bytes 3145732

commit v3 on v2

--- a/solution.py
+++ b/solution.py
@@ -18,6 +18,8 @@
 BF = jnp.bfloat16
 F32 = jnp.float32
 VMEM = pl.BlockSpec(memory_space=pltpu.VMEM)
+ANY = pl.BlockSpec(memory_space=pl.ANY)
+PARTS = 4
 STEPS = (0, 4, 1, 5, 7, 3, 2, 6)
 NT = (((1,), (1,)), ((), ()))
 
@@ -34,30 +36,47 @@
     return jnp.dot(a, b, preferred_element_type=F32)
 
 
-def pack_kernel(rows_ref, owner_ref, list_ref, pay_ref, pos_ref):
+def pack_kernel(rows_hbm, owner_hbm, list_hbm, pay_hbm, pos_hbm, rows_ref, owner_ref, list_ref, pay_ref, pos_ref, sems, sent_sems):
+    fetch = [
+        pltpu.make_async_copy(owner_hbm, owner_ref, sems.at[0]),
+        pltpu.make_async_copy(list_hbm, list_ref, sems.at[1]),
+        pltpu.make_async_copy(rows_hbm, rows_ref, sems.at[2]),
+    ]
+    for copy in fetch:
+        copy.start()
     rows = rows_ref.shape[0]
+    upto = ones_where(iota((rows, rows), 0) <= iota((rows, rows), 1))
+    fetch[0].wait()
     owner = owner_ref[...]
     mine = iota((PEERS, rows), 0) == owner
-    upto = ones_where(iota((rows, rows), 0) <= iota((rows, rows), 1))
     count = dot(ones_where(mine), upto)
     rank = jnp.sum(jnp.where(mine, count, 0.0), axis=0, keepdims=True).astype(jnp.int32) - 1
     pos = owner * CAP + rank
     pos_ref[...] = pos
-    half = SLOTS // 2
-    for part in range(2):
-        place = ones_where(iota((half, rows), 0) + part * half == pos)
-        sent = dot(place, rows_ref[...]).astype(BF)
-        peers = pl.ds(part * (PEERS // 2), PEERS // 2)
-        for c in range(COLS):
-            pay_ref[peers, c * CAP : (c + 1) * CAP, :] = sent[:, c * LANES : (c + 1) * LANES].reshape(
-                PEERS // 2, CAP, LANES
-            )
+    leave = [pltpu.make_async_copy(pos_ref, pos_hbm, sems.at[3])]
+    leave[0].start()
+    fetch[1].wait()
     tags = jnp.where(mine, (list_ref[...] + 1).astype(F32), 0.0).astype(BF)
     at_rank = ones_where(iota((LANES, rows), 0) == rank)
     tag_rows = lax.dot_general(tags, at_rank, NT, preferred_element_type=F32)
     pay_ref[:, COLS * CAP :, :] = jnp.broadcast_to(
         tag_rows[:, None, :], (PEERS, PAY - COLS * CAP, LANES)
     ).astype(BF)
+    fetch[2].wait()
+    for part in range(PARTS):
+        width = SLOTS // PARTS
+        place = ones_where(iota((width, rows), 0) + part * width == pos)
+        sent = dot(place, rows_ref[...]).astype(BF)
+        peers = pl.ds(part * (PEERS // PARTS), PEERS // PARTS)
+        for c in range(COLS):
+            pay_ref[peers, c * CAP : (c + 1) * CAP, :] = sent[:, c * LANES : (c + 1) * LANES].reshape(
+                PEERS // PARTS, CAP, LANES
+            )
+        copy = pltpu.make_async_copy(pay_ref.at[peers], pay_hbm.at[peers], sent_sems.at[part])
+        copy.start()
+        leave.append(copy)
+    for copy in leave:
+        copy.wait()
 
 
 def pack(rows, owner, lists):
@@ -67,8 +86,17 @@
             jax.ShapeDtypeStruct((PEERS, PAY, LANES), BF),
             jax.ShapeDtypeStruct(owner.shape, jnp.int32),
         ),
-        in_specs=[VMEM] * 3,
-        out_specs=(VMEM, VMEM),
+        in_specs=[ANY] * 3,
+        out_specs=(ANY, ANY),
+        scratch_shapes=[
+            pltpu.VMEM(rows.shape, BF),
+            pltpu.VMEM(owner.shape, jnp.int32),
+            pltpu.VMEM(lists.shape, jnp.int32),
+            pltpu.VMEM((PEERS, PAY, LANES), BF),
+            pltpu.VMEM(owner.shape, jnp.int32),
+            pltpu.SemaphoreType.DMA((4,)),
+            pltpu.SemaphoreType.DMA((PARTS,)),
+        ],
         name="pack_rows",
         cost_estimate=pl.CostEstimate(flops=2**29, bytes_accessed=2**21, transcendentals=0),
     )(rows, owner, lists)

time: 103 us -> 103 us (level)
  no operation moved by 1% of the time
where the time goes in v3:
time: 103 us; the launch traced here: 102 us
  starting transfers between devices  38 us (37%)
  blocking collectives  33.2 us (32%)
  Pallas kernels  19.8 us (19%)
  waiting for transfers between devices  9.62 us (9%)
  matrix products  1.5 us (1%)
    all_to_all x1, blocking collectives, exchange(): lax.all_to_all(values, 'cand', split_axis=0, concat_axis=0, tiled=True)  33.2 us
    pallas_call x1, Pallas kernels, rerank(): pl.pallas_call(main_kernel, out_shape=jax.ShapeDtypeStruct((SLOTS, D), BF...  15.1 us
    all_to_all x1, starting transfers between devices, exchange(): lax.all_to_all(values, 'cand', split_axis=0, concat_axis=0, tiled=True)  12.6 us
    ppermute x4, starting transfers between devices, gather_projection(): return near + tuple((lax.ppermute(piece, 'req', CORE) for piece in near))  8.34 us
    ppermute x1, starting transfers between devices, local(): opposite = lax.ppermute(project_in, 'req', along_y(4))  7.72 us
    all_to_all x1, waiting for transfers between devices, exchange(): lax.all_to_all(values, 'cand', split_axis=0, concat_axis=0, tiled=True)  6.1 us
    ppermute x1, starting transfers between devices, gather_projection(): one = lax.ppermute(pair, 'req', along_y(7))  3.57 us
    ppermute x1, starting transfers between devices, gather_projection(): seven = lax.ppermute(pair, 'req', along_y(1))  3.49 us
  transfers between devices with their start and end apart: 9, of which 3 were waited for; matrix products, arithmetic and copies ran while one was open for 0% of the time, Pallas kernels for 5%

profile of v3, /device:TPU:64, one launch (start us, length us, event | category | flops | bytes accessed | tf_op | source)
XLA Modules:
  0.0 102.5 jit_solution(833031086732453115)
XLA Ops:
  0.0 7.7 %collective-permute-start = (bf16[32,1536]{1,0:T(8,128)(2,1)}, bf16[32,1536]{1,0:T(8,128)(2,1)S(1)}, u32[]{:S(2)}, u32[]{:S(2)}) collective-permute-start(bf16[32,1536]{1,0:T(8,128)(2,1)} %param.16), channel_id=1, source_target_pairs={{0,256},{32,288},{64,320},{96,352},{128,384},{160,416},{192,448},{... | collective-permute-start | bytes 294920 | tf_op jit(solution)/shard_map/ppermute | solution.py:284
  7.7 2.6 %pack_rows.1 = (bf16[32,136,128]{2,1,0:T(8,128)(2,1)}, s32[1,512]{1,0:T(1,128)}) custom-call(bf16[512,512]{1,0:T(8,128)(2,1)} %bitcast.14, s32[1,512]{1,0:T(1,128)} %bitcast.15, s32[1,512]{1,0:T(1,128)} %list_hbm.1), custom_call_target="tpu_custom_call" | custom-call | flops 536870912 | bytes 2097152 | tf_op jit(solution)/shard_map/pack_rows/pallas_call | solution.py:83
  10.3 12.6 %all-to-all-start = ((bf16[32,136,128]{2,1,0:T(8,128)(2,1)}), bf16[32,136,128]{2,1,0:T(8,128)(2,1)}, u32[]{:S(2)}, u32[]{:S(2)}) async-start(bf16[32,136,128]{2,1,0:T(8,128)(2,1)} %get-tuple-element.11), calls=%async_computation | async-start | bytes 2228224 | tf_op jit(solution)/shard_map/all_to_all | solution.py:254
  23.0 0.0 copy-start.5
  23.0 0.0 copy-start
  23.0 0.0 copy-start.1
  23.0 0.0 copy-start.2
  23.0 0.0 copy-start.3
  23.1 0.0 copy-start.4
  23.1 2.1 %pick_matrix.1 = bf16[512,1024]{1,0:T(8,128)(2,1)} custom-call(s32[1,512]{1,0:T(1,128)} %get-tuple-element.9.pos_ref), custom_call_target="tpu_custom_call" | custom-call | flops 68719476736 | bytes 268435456 | tf_op jit(solution)/shard_map/pick_matrix/pallas_call | solution.py:115
  25.2 0.0 copy-done.5
  25.2 0.0 collective-permute-done
  25.2 2.2 %collective-permute-start.3 = (bf16[64,1536]{1,0:T(8,128)(2,1)S(1)}, bf16[64,1536]{1,0:T(8,128)(2,1)S(1)}, u32[]{:S(2)}, u32[]{:S(2)}) collective-permute-start(bf16[64,1536]{1,0:T(8,128)(2,1)S(1)} %constant_dynamic-update-slice_fusion.refs_0_), channel_id=1, source_target_pairs={{0,384},{32,416},{64,448},{96,480},{128,0},{160,32},{192,64},{224,... | collective-permute-start | bytes 589832 | tf_op jit(solution)/shard_map/ppermute | solution.py:266
  27.5 3.5 %collective-permute-start.2 = (bf16[64,1536]{1,0:T(8,128)(2,1)S(1)}, bf16[64,1536]{1,0:T(8,128)(2,1)}, u32[]{:S(2)}, u32[]{:S(2)}) collective-permute-start(bf16[64,1536]{1,0:T(8,128)(2,1)S(1)} %constant_dynamic-update-slice_fusion.refs_0_), channel_id=1, source_target_pairs={{0,64},{32,96},{64,128},{96,160},{128,192},{160,224},{192,256},{22... | collective-permute-start | bytes 589832 | tf_op jit(solution)/shard_map/ppermute | solution.py:268
  31.0 3.6 %collective-permute-start.1 = (bf16[64,1536]{1,0:T(8,128)(2,1)S(1)}, bf16[64,1536]{1,0:T(8,128)(2,1)}, u32[]{:S(2)}, u32[]{:S(2)}) collective-permute-start(bf16[64,1536]{1,0:T(8,128)(2,1)S(1)} %constant_dynamic-update-slice_fusion.refs_0_), channel_id=1, source_target_pairs={{0,448},{32,480},{64,0},{96,32},{128,64},{160,96},{192,128},{224,1... | collective-permute-start | bytes 589832 | tf_op jit(solution)/shard_map/ppermute | solution.py:267
  34.5 1.9 %collective-permute-start.4 = (bf16[64,1536]{1,0:T(8,128)(2,1)S(1)}, bf16[64,1536]{1,0:T(8,128)(2,1)}, u32[]{:S(2)}, u32[]{:S(2)}) collective-permute-start(bf16[64,1536]{1,0:T(8,128)(2,1)S(1)} %constant_dynamic-update-slice_fusion.refs_0_), channel_id=1, source_target_pairs={{0,32},{32,0},{64,96},{96,64},{128,160},{160,128},{192,224},{224,1... | collective-permute-start | bytes 589832 | tf_op jit(solution)/shard_map/ppermute | solution.py:270
  36.5 2.0 %collective-permute-done.3.refs_3_ = bf16[64,1536]{1,0:T(8,128)(2,1)S(1)} collective-permute-done((bf16[64,1536]{1,0:T(8,128)(2,1)S(1)}, bf16[64,1536]{1,0:T(8,128)(2,1)S(1)}, u32[]{:S(2)}, u32[]{:S(2)}) %collective-permute-start.3) | collective-permute-done | bytes 196640 | tf_op jit(solution)/shard_map/ppermute | solution.py:266
  38.5 1.9 %collective-permute-start.7 = (bf16[64,1536]{1,0:T(8,128)(2,1)S(1)}, bf16[64,1536]{1,0:T(8,128)(2,1)}, u32[]{:S(2)}, u32[]{:S(2)}) collective-permute-start(bf16[64,1536]{1,0:T(8,128)(2,1)S(1)} %collective-permute-done.3.refs_3_), channel_id=1, source_target_pairs={{0,32},{32,0},{64,96},{96,64},{128,160},{160,128},{192,224},{224,1... | collective-permute-start | bytes 589832 | tf_op jit(solution)/shard_map/ppermute | solution.py:270
  40.4 0.0 collective-permute-done.2.refs_2_
  40.4 2.4 %collective-permute-start.6 = (bf16[64,1536]{1,0:T(8,128)(2,1)}, bf16[64,1536]{1,0:T(8,128)(2,1)}, u32[]{:S(2)}, u32[]{:S(2)}) collective-permute-start(bf16[64,1536]{1,0:T(8,128)(2,1)} %collective-permute-done.2.refs_2_), channel_id=1, source_target_pairs={{0,32},{32,0},{64,96},{96,64},{128,160},{160,128},{192,224},{224,1... | collective-permute-start | bytes 589832 | tf_op jit(solution)/shard_map/ppermute | solution.py:270
  42.8 0.0 collective-permute-done.1.refs_1_
  42.9 2.1 %collective-permute-start.5 = (bf16[64,1536]{1,0:T(8,128)(2,1)}, bf16[64,1536]{1,0:T(8,128)(2,1)}, u32[]{:S(2)}, u32[]{:S(2)}) collective-permute-start(bf16[64,1536]{1,0:T(8,128)(2,1)} %collective-permute-done.1.refs_1_), channel_id=1, source_target_pairs={{0,32},{32,0},{64,96},{96,64},{128,160},{160,128},{192,224},{224,1... | collective-permute-start | bytes 589832 | tf_op jit(solution)/shard_map/ppermute | solution.py:270
  45.0 0.1 pad_add_fusion.y_ref
  45.1 0.0 collective-permute-done.4.refs_4_
  45.1 0.0 collective-permute-done.7.refs_7_
  45.1 0.0 collective-permute-done.6.refs_6_
  45.1 1.5 %collective-permute-done.5.refs_5_ = bf16[64,1536]{1,0:T(8,128)(2,1)} collective-permute-done((bf16[64,1536]{1,0:T(8,128)(2,1)}, bf16[64,1536]{1,0:T(8,128)(2,1)}, u32[]{:S(2)}, u32[]{:S(2)}) %collective-permute-start.5) | collective-permute-done | bytes 196640 | tf_op jit(solution)/shard_map/ppermute | solution.py:270
  46.5 6.1 %all-to-all-done.pay_ref = bf16[32,136,128]{2,1,0:T(8,128)(2,1)} async-done(((bf16[32,136,128]{2,1,0:T(8,128)(2,1)}), bf16[32,136,128]{2,1,0:T(8,128)(2,1)}, u32[]{:S(2)}, u32[]{:S(2)}) %all-to-all-start) | async-done | bytes 1114144 | tf_op jit(solution)/shard_map/all_to_all | solution.py:254
  52.6 0.0 copy-done
  52.7 15.1 %rerank_lists.1 = bf16[1024,512]{1,0:T(8,128)(2,1)S(1)} custom-call(s32[2]{0:T(128)S(1)} %pad_add_fusion.y_ref, bf16[32,136,128]{2,1,0:T(8,128)(2,1)} %all-to-all-done.pay_ref, bf16[2,512]{1,0:T(2,128)(2,1)S(1)} %bitcast.12, bf16[512,512]{1,0:T(8,128)(2,1)S(1)} %copy-done.2, bf16[512,1024]{1,0:T(8,128)(2,1)S(1)} %copy-done, bf16[1024,512]{1,0:T(8,128)(2,1)S(1)} %copy-done.1, ...), custom_call_target="tpu_custom_call" | custom-call | flops 17179869184 | bytes 8388608 | tf_op jit(solution)/shard_map/rerank_lists/pallas_call | solution.py:232
  67.8 33.2 %all_to_all.10 = bf16[32,32,512]{2,1,0:T(8,128)(2,1)S(1)} all-to-all(bf16[32,32,512]{2,1,0:T(8,128)(2,1)S(1)} %bitcast.11), channel_id=1, replica_groups=mesh['req'=16,'cand'=32] {'cand'}, dimensions={0} | all-to-all | bytes 2097152 | tf_op jit(solution)/shard_map/all_to_all | solution.py:254
  101.0 1.5 %fusion = bf16[1,512,512]{2,1,0:T(8,128)(2,1)} fusion(bf16[512,1024]{1,0:T(8,128)(2,1)S(1)} %copy-done.6, bf16[1024,512]{1,0:T(8,128)(2,1)S(1)} %bitcast.13), kind=kOutput, calls=%fused_computation.1 | convolution fusion | flops 537133056 | bytes 2621440 | tf_op jit(solution)/shard_map/dot_general | solution.py:36
  (8 shorter events, 0.0 us)
Async XLA Ops:
  0.0 25.2 %collective-permute-start = (bf16[32,1536]{1,0:T(8,128)(2,1)}, bf16[32,1536]{1,0:T(8,128)(2,1)S(1)}, u32[]{:S(2)}, u32[]{:S(2)}) collective-permute-start(bf16[32,1536]{1,0:T(8,128)(2,1)} %param.16), channel_id=1, source_target_pairs={{0,256},{32,288},{64,320},{96,352},{128,384},{160,416},{192,448},{... | collective-permute-start | bytes 294920 | tf_op jit(solution)/shard_map/ppermute | solution.py:284
  10.3 42.3 %all-to-all-start = ((bf16[32,136,128]{2,1,0:T(8,128)(2,1)}), bf16[32,136,128]{2,1,0:T(8,128)(2,1)}, u32[]{:S(2)}, u32[]{:S(2)}) async-start(bf16[32,136,128]{2,1,0:T(8,128)(2,1)} %get-tuple-element.11), calls=%async_computation | async-start | bytes 2228224 | tf_op jit(solution)/shard_map/all_to_all | solution.py:254
  23.0 2.2 %copy-start.5 = (bf16[32,1536]{1,0:T(8,128)(2,1)S(1)}, bf16[32,1536]{1,0:T(8,128)(2,1)}, u32[]{:S(2)}) copy-start(bf16[32,1536]{1,0:T(8,128)(2,1)} %param.16) | copy-start | bytes 294916
  23.0 29.6 %copy-start = (bf16[512,1024]{1,0:T(8,128)(2,1)S(1)}, bf16[512,1024]{1,0:T(8,128)(2,1)}, u32[]{:S(2)}) copy-start(bf16[512,1024]{1,0:T(8,128)(2,1)} %up_ref.1) | copy-start | bytes 3145732
  23.0 29.6 %copy-start.1 = (bf16[1024,512]{1,0:T(8,128)(2,1)S(1)}, bf16[1024,512]{1,0:T(8,128)(2,1)}, u32[]{:S(2)}) copy-start(bf16[1024,512]{1,0:T(8,128)(2,1)} %down_ref.1) | copy-start | bytes 3145732
  23.0 29.6 %copy-start.2 = (bf16[512,512]{1,0:T(8,128)(2,1)S(1)}, bf16[512,512]{1,0:T(8,128)(2,1)}, u32[]{:S(2)}) copy-start(bf16[512,512]{1,0:T(8,128)(2,1)} %cross_ref.1) | copy-start | bytes 1572868
  23.0 29.6 %copy-start.3 = (bf16[512,512]{1,0:T(8,128)(2,1)S(1)}, bf16[512,512]{1,0:T(8,128)(2,1)}, u32[]{:S(2)}) copy-start(bf16[512,512]{1,0:T(8,128)(2,1)} %refs_8_.1) | copy-start | bytes 1572868
  23.1 29.6 %copy-start.4 = (bf16[1,2,512]{2,1,0:T(2,128)(2,1)S(1)}, bf16[1,2,512]{2,1,0:T(2,128)(2,1)}, u32[]{:S(2)}) copy-start(bf16[1,2,512]{2,1,0:T(2,128)(2,1)} %param.10) | copy-start | bytes 6148
  25.2 13.3 %collective-permute-start.3 = (bf16[64,1536]{1,0:T(8,128)(2,1)S(1)}, bf16[64,1536]{1,0:T(8,128)(2,1)S(1)}, u32[]{:S(2)}, u32[]{:S(2)}) collective-permute-start(bf16[64,1536]{1,0:T(8,128)(2,1)S(1)} %constant_dynamic-update-slice_fusion.refs_0_), channel_id=1, source_target_pairs={{0,384},{32,416},{64,448},{96,480},{128,0},{160,32},{192,64},{224,... | collective-permute-start | bytes 589832 | tf_op jit(solution)/shard_map/ppermute | solution.py:266
  27.5 13.0 %collective-permute-start.2 = (bf16[64,1536]{1,0:T(8,128)(2,1)S(1)}, bf16[64,1536]{1,0:T(8,128)(2,1)}, u32[]{:S(2)}, u32[]{:S(2)}) collective-permute-start(bf16[64,1536]{1,0:T(8,128)(2,1)S(1)} %constant_dynamic-update-slice_fusion.refs_0_), channel_id=1, source_target_pairs={{0,64},{32,96},{64,128},{96,160},{128,192},{160,224},{192,256},{22... | collective-permute-start | bytes 589832 | tf_op jit(solution)/shard_map/ppermute | solution.py:268
  31.0 11.9 %collective-permute-start.1 = (bf16[64,1536]{1,0:T(8,128)(2,1)S(1)}, bf16[64,1536]{1,0:T(8,128)(2,1)}, u32[]{:S(2)}, u32[]{:S(2)}) collective-permute-start(bf16[64,1536]{1,0:T(8,128)(2,1)S(1)} %constant_dynamic-update-slice_fusion.refs_0_), channel_id=1, source_target_pairs={{0,448},{32,480},{64,0},{96,32},{128,64},{160,96},{192,128},{224,1... | collective-permute-start | bytes 589832 | tf_op jit(solution)/shard_map/ppermute | solution.py:267
  34.5 10.5 %collective-permute-start.4 = (bf16[64,1536]{1,0:T(8,128)(2,1)S(1)}, bf16[64,1536]{1,0:T(8,128)(2,1)}, u32[]{:S(2)}, u32[]{:S(2)}) collective-permute-start(bf16[64,1536]{1,0:T(8,128)(2,1)S(1)} %constant_dynamic-update-slice_fusion.refs_0_), channel_id=1, source_target_pairs={{0,32},{32,0},{64,96},{96,64},{128,160},{160,128},{192,224},{224,1... | collective-permute-start | bytes 589832 | tf_op jit(solution)/shard_map/ppermute | solution.py:270
  38.5 6.6 %collective-permute-start.7 = (bf16[64,1536]{1,0:T(8,128)(2,1)S(1)}, bf16[64,1536]{1,0:T(8,128)(2,1)}, u32[]{:S(2)}, u32[]{:S(2)}) collective-permute-start(bf16[64,1536]{1,0:T(8,128)(2,1)S(1)} %collective-permute-done.3.refs_3_), channel_id=1, source_target_pairs={{0,32},{32,0},{64,96},{96,64},{128,160},{160,128},{192,224},{224,1... | collective-permute-start | bytes 589832 | tf_op jit(solution)/shard_map/ppermute | solution.py:270
  40.4 4.6 %collective-permute-start.6 = (bf16[64,1536]{1,0:T(8,128)(2,1)}, bf16[64,1536]{1,0:T(8,128)(2,1)}, u32[]{:S(2)}, u32[]{:S(2)}) collective-permute-start(bf16[64,1536]{1,0:T(8,128)(2,1)} %collective-permute-done.2.refs_2_), channel_id=1, source_target_pairs={{0,32},{32,0},{64,96},{96,64},{128,160},{160,128},{192,224},{224,1... | collective-permute-start | bytes 589832 | tf_op jit(solution)/shard_map/ppermute | solution.py:270
  42.9 3.7 %collective-permute-start.5 = (bf16[64,1536]{1,0:T(8,128)(2,1)}, bf16[64,1536]{1,0:T(8,128)(2,1)}, u32[]{:S(2)}, u32[]{:S(2)}) collective-permute-start(bf16[64,1536]{1,0:T(8,128)(2,1)} %collective-permute-done.1.refs_1_), channel_id=1, source_target_pairs={{0,32},{32,0},{64,96},{96,64},{128,160},{160,128},{192,224},{224,1... | collective-permute-start | bytes 589832 | tf_op jit(solution)/shard_map/ppermute | solution.py:270
  67.8 33.2 %copy-start.6 = (bf16[512,1024]{1,0:T(8,128)(2,1)S(1)}, bf16[512,1024]{1,0:T(8,128)(2,1)}, u32[]{:S(2)}) copy-start(bf16[512,1024]{1,0:T(8,128)(2,1)} %pick_matrix.1) | copy-start | bytes 3145732

commit v4 on v3

--- a/solution.py
+++ b/solution.py
@@ -141,8 +141,6 @@
             spot = pl.multiple_of((chip + which) * share, share)
             in_ref[pl.ds(spot, share), :] = ref[i % 2 * share : (i % 2 + 1) * share, :]
 
-    in_t[...] = jnp.concatenate([in_ref[:, :D].T, in_ref[:, 2 * D :].T], axis=0)
-
     head = D // HEADS
     lane = iota((SLOTS, LANES), 1)
     low = lane < head
@@ -171,6 +169,7 @@
     mixed = (crossed.astype(F32) + dot(active, down_ref[...])).astype(BF)
     mixed_ref[...] = mixed
 
+    in_t[...] = jnp.concatenate([in_ref[:, :D].T, in_ref[:, 2 * D :].T], axis=0)
     keys = dot(mixed, in_ref[:, D : 2 * D])
     square = (keys * keys).astype(BF)
     spot = lax.rem(lane, head)
@@ -218,7 +217,7 @@
                 cut = slice(j * QBLOCK, (j + 1) * QBLOCK)
                 powered = jnp.exp(dot(k[p], queries_ref[h, :, cut])).astype(BF)
                 summed = dot(values_ref[h], powered)
-                halves.append((summed[:head] / summed[head : head + 1]).astype(BF))
+                halves.append((summed[:head] * (1.0 / summed[head : head + 1])).astype(BF))
             pair.append(jnp.concatenate(halves, axis=1))
         attended_ref[p] = jnp.concatenate(pair, axis=0).T
 

time: 103 us -> 103 us (level)
  no operation moved by 1% of the time
where the time goes in v4:
time: 103 us; the launch traced here: 102 us
  starting transfers between devices  38 us (37%)
  blocking collectives  33.2 us (32%)
  Pallas kernels  19.8 us (19%)
  waiting for transfers between devices  9.62 us (9%)
  matrix products  1.5 us (1%)
    all_to_all x1, blocking collectives, exchange(): lax.all_to_all(values, 'cand', split_axis=0, concat_axis=0, tiled=True)  33.2 us
    pallas_call x1, Pallas kernels, rerank(): pl.pallas_call(main_kernel, out_shape=jax.ShapeDtypeStruct((SLOTS, D), BF...  15.1 us
    all_to_all x1, starting transfers between devices, exchange(): lax.all_to_all(values, 'cand', split_axis=0, concat_axis=0, tiled=True)  12.6 us
    ppermute x4, starting transfers between devices, gather_projection(): return near + tuple((lax.ppermute(piece, 'req', CORE) for piece in near))  8.34 us
    ppermute x1, starting transfers between devices, local(): opposite = lax.ppermute(project_in, 'req', along_y(4))  7.72 us
    all_to_all x1, waiting for transfers between devices, exchange(): lax.all_to_all(values, 'cand', split_axis=0, concat_axis=0, tiled=True)  6.1 us
    ppermute x1, starting transfers between devices, gather_projection(): one = lax.ppermute(pair, 'req', along_y(7))  3.57 us
    ppermute x1, starting transfers between devices, gather_projection(): seven = lax.ppermute(pair, 'req', along_y(1))  3.49 us
  transfers between devices with their start and end apart: 9, of which 3 were waited for; matrix products, arithmetic and copies ran while one was open for 0% of the time, Pallas kernels for 5%

profile of v4, /device:TPU:64, one launch (start us, length us, event | category | flops | bytes accessed | tf_op | source)
XLA Modules:
  0.0 102.5 jit_solution(13201191075516637531)
XLA Ops:
  0.0 7.7 %collective-permute-start = (bf16[32,1536]{1,0:T(8,128)(2,1)}, bf16[32,1536]{1,0:T(8,128)(2,1)S(1)}, u32[]{:S(2)}, u32[]{:S(2)}) collective-permute-start(bf16[32,1536]{1,0:T(8,128)(2,1)} %param.16), channel_id=1, source_target_pairs={{0,256},{32,288},{64,320},{96,352},{128,384},{160,416},{192,448},{... | collective-permute-start | bytes 294920 | tf_op jit(solution)/shard_map/ppermute | solution.py:283
  7.7 2.6 %pack_rows.1 = (bf16[32,136,128]{2,1,0:T(8,128)(2,1)}, s32[1,512]{1,0:T(1,128)}) custom-call(bf16[512,512]{1,0:T(8,128)(2,1)} %bitcast.14, s32[1,512]{1,0:T(1,128)} %bitcast.15, s32[1,512]{1,0:T(1,128)} %list_hbm.1), custom_call_target="tpu_custom_call" | custom-call | flops 536870912 | bytes 2097152 | tf_op jit(solution)/shard_map/pack_rows/pallas_call | solution.py:83
  10.3 12.6 %all-to-all-start = ((bf16[32,136,128]{2,1,0:T(8,128)(2,1)}), bf16[32,136,128]{2,1,0:T(8,128)(2,1)}, u32[]{:S(2)}, u32[]{:S(2)}) async-start(bf16[32,136,128]{2,1,0:T(8,128)(2,1)} %get-tuple-element.11), calls=%async_computation | async-start | bytes 2228224 | tf_op jit(solution)/shard_map/all_to_all | solution.py:253
  23.0 0.0 copy-start.5
  23.0 0.0 copy-start
  23.0 0.0 copy-start.1
  23.0 0.0 copy-start.2
  23.0 0.0 copy-start.3
  23.1 0.0 copy-start.4
  23.1 2.1 %pick_matrix.1 = bf16[512,1024]{1,0:T(8,128)(2,1)} custom-call(s32[1,512]{1,0:T(1,128)} %get-tuple-element.9.pos_ref), custom_call_target="tpu_custom_call" | custom-call | flops 68719476736 | bytes 268435456 | tf_op jit(solution)/shard_map/pick_matrix/pallas_call | solution.py:115
  25.2 0.0 copy-done.5
  25.2 0.0 collective-permute-done
  25.2 2.2 %collective-permute-start.3 = (bf16[64,1536]{1,0:T(8,128)(2,1)S(1)}, bf16[64,1536]{1,0:T(8,128)(2,1)S(1)}, u32[]{:S(2)}, u32[]{:S(2)}) collective-permute-start(bf16[64,1536]{1,0:T(8,128)(2,1)S(1)} %constant_dynamic-update-slice_fusion.refs_0_), channel_id=1, source_target_pairs={{0,384},{32,416},{64,448},{96,480},{128,0},{160,32},{192,64},{224,... | collective-permute-start | bytes 589832 | tf_op jit(solution)/shard_map/ppermute | solution.py:265
  27.5 3.5 %collective-permute-start.2 = (bf16[64,1536]{1,0:T(8,128)(2,1)S(1)}, bf16[64,1536]{1,0:T(8,128)(2,1)}, u32[]{:S(2)}, u32[]{:S(2)}) collective-permute-start(bf16[64,1536]{1,0:T(8,128)(2,1)S(1)} %constant_dynamic-update-slice_fusion.refs_0_), channel_id=1, source_target_pairs={{0,64},{32,96},{64,128},{96,160},{128,192},{160,224},{192,256},{22... | collective-permute-start | bytes 589832 | tf_op jit(solution)/shard_map/ppermute | solution.py:267
  31.0 3.6 %collective-permute-start.1 = (bf16[64,1536]{1,0:T(8,128)(2,1)S(1)}, bf16[64,1536]{1,0:T(8,128)(2,1)}, u32[]{:S(2)}, u32[]{:S(2)}) collective-permute-start(bf16[64,1536]{1,0:T(8,128)(2,1)S(1)} %constant_dynamic-update-slice_fusion.refs_0_), channel_id=1, source_target_pairs={{0,448},{32,480},{64,0},{96,32},{128,64},{160,96},{192,128},{224,1... | collective-permute-start | bytes 589832 | tf_op jit(solution)/shard_map/ppermute | solution.py:266
  34.5 1.9 %collective-permute-start.4 = (bf16[64,1536]{1,0:T(8,128)(2,1)S(1)}, bf16[64,1536]{1,0:T(8,128)(2,1)}, u32[]{:S(2)}, u32[]{:S(2)}) collective-permute-start(bf16[64,1536]{1,0:T(8,128)(2,1)S(1)} %constant_dynamic-update-slice_fusion.refs_0_), channel_id=1, source_target_pairs={{0,32},{32,0},{64,96},{96,64},{128,160},{160,128},{192,224},{224,1... | collective-permute-start | bytes 589832 | tf_op jit(solution)/shard_map/ppermute | solution.py:269
  36.5 2.0 %collective-permute-done.3.refs_3_ = bf16[64,1536]{1,0:T(8,128)(2,1)S(1)} collective-permute-done((bf16[64,1536]{1,0:T(8,128)(2,1)S(1)}, bf16[64,1536]{1,0:T(8,128)(2,1)S(1)}, u32[]{:S(2)}, u32[]{:S(2)}) %collective-permute-start.3) | collective-permute-done | bytes 196640 | tf_op jit(solution)/shard_map/ppermute | solution.py:265
  38.5 1.9 %collective-permute-start.7 = (bf16[64,1536]{1,0:T(8,128)(2,1)S(1)}, bf16[64,1536]{1,0:T(8,128)(2,1)}, u32[]{:S(2)}, u32[]{:S(2)}) collective-permute-start(bf16[64,1536]{1,0:T(8,128)(2,1)S(1)} %collective-permute-done.3.refs_3_), channel_id=1, source_target_pairs={{0,32},{32,0},{64,96},{96,64},{128,160},{160,128},{192,224},{224,1... | collective-permute-start | bytes 589832 | tf_op jit(solution)/shard_map/ppermute | solution.py:269
  40.4 0.0 collective-permute-done.2.refs_2_
  40.4 2.4 %collective-permute-start.6 = (bf16[64,1536]{1,0:T(8,128)(2,1)}, bf16[64,1536]{1,0:T(8,128)(2,1)}, u32[]{:S(2)}, u32[]{:S(2)}) collective-permute-start(bf16[64,1536]{1,0:T(8,128)(2,1)} %collective-permute-done.2.refs_2_), channel_id=1, source_target_pairs={{0,32},{32,0},{64,96},{96,64},{128,160},{160,128},{192,224},{224,1... | collective-permute-start | bytes 589832 | tf_op jit(solution)/shard_map/ppermute | solution.py:269
  42.8 0.0 collective-permute-done.1.refs_1_
  42.9 2.1 %collective-permute-start.5 = (bf16[64,1536]{1,0:T(8,128)(2,1)}, bf16[64,1536]{1,0:T(8,128)(2,1)}, u32[]{:S(2)}, u32[]{:S(2)}) collective-permute-start(bf16[64,1536]{1,0:T(8,128)(2,1)} %collective-permute-done.1.refs_1_), channel_id=1, source_target_pairs={{0,32},{32,0},{64,96},{96,64},{128,160},{160,128},{192,224},{224,1... | collective-permute-start | bytes 589832 | tf_op jit(solution)/shard_map/ppermute | solution.py:269
  45.0 0.1 pad_add_fusion.y_ref
  45.1 0.0 collective-permute-done.4.refs_4_
  45.1 0.0 collective-permute-done.7.refs_7_
  45.1 0.0 collective-permute-done.6.refs_6_
  45.1 1.5 %collective-permute-done.5.refs_5_ = bf16[64,1536]{1,0:T(8,128)(2,1)} collective-permute-done((bf16[64,1536]{1,0:T(8,128)(2,1)}, bf16[64,1536]{1,0:T(8,128)(2,1)}, u32[]{:S(2)}, u32[]{:S(2)}) %collective-permute-start.5) | collective-permute-done | bytes 196640 | tf_op jit(solution)/shard_map/ppermute | solution.py:269
  46.5 6.1 %all-to-all-done.pay_ref = bf16[32,136,128]{2,1,0:T(8,128)(2,1)} async-done(((bf16[32,136,128]{2,1,0:T(8,128)(2,1)}), bf16[32,136,128]{2,1,0:T(8,128)(2,1)}, u32[]{:S(2)}, u32[]{:S(2)}) %all-to-all-start) | async-done | bytes 1114144 | tf_op jit(solution)/shard_map/all_to_all | solution.py:253
  52.6 0.0 copy-done
  52.7 15.1 %rerank_lists.1 = bf16[1024,512]{1,0:T(8,128)(2,1)S(1)} custom-call(s32[2]{0:T(128)S(1)} %pad_add_fusion.y_ref, bf16[32,136,128]{2,1,0:T(8,128)(2,1)} %all-to-all-done.pay_ref, bf16[2,512]{1,0:T(2,128)(2,1)S(1)} %bitcast.12, bf16[512,512]{1,0:T(8,128)(2,1)S(1)} %copy-done.2, bf16[512,1024]{1,0:T(8,128)(2,1)S(1)} %copy-done, bf16[1024,512]{1,0:T(8,128)(2,1)S(1)} %copy-done.1, ...), custom_call_target="tpu_custom_call" | custom-call | flops 17179869184 | bytes 8388608 | tf_op jit(solution)/shard_map/rerank_lists/pallas_call | solution.py:231
  67.8 33.2 %all_to_all.10 = bf16[32,32,512]{2,1,0:T(8,128)(2,1)S(1)} all-to-all(bf16[32,32,512]{2,1,0:T(8,128)(2,1)S(1)} %bitcast.11), channel_id=1, replica_groups=mesh['req'=16,'cand'=32] {'cand'}, dimensions={0} | all-to-all | bytes 2097152 | tf_op jit(solution)/shard_map/all_to_all | solution.py:253
  101.0 1.5 %fusion = bf16[1,512,512]{2,1,0:T(8,128)(2,1)} fusion(bf16[512,1024]{1,0:T(8,128)(2,1)S(1)} %copy-done.6, bf16[1024,512]{1,0:T(8,128)(2,1)S(1)} %bitcast.13), kind=kOutput, calls=%fused_computation.1 | convolution fusion | flops 537133056 | bytes 2621440 | tf_op jit(solution)/shard_map/dot_general | solution.py:36
  (8 shorter events, 0.0 us)
Async XLA Ops:
  0.0 25.2 %collective-permute-start = (bf16[32,1536]{1,0:T(8,128)(2,1)}, bf16[32,1536]{1,0:T(8,128)(2,1)S(1)}, u32[]{:S(2)}, u32[]{:S(2)}) collective-permute-start(bf16[32,1536]{1,0:T(8,128)(2,1)} %param.16), channel_id=1, source_target_pairs={{0,256},{32,288},{64,320},{96,352},{128,384},{160,416},{192,448},{... | collective-permute-start | bytes 294920 | tf_op jit(solution)/shard_map/ppermute | solution.py:283
  10.3 42.3 %all-to-all-start = ((bf16[32,136,128]{2,1,0:T(8,128)(2,1)}), bf16[32,136,128]{2,1,0:T(8,128)(2,1)}, u32[]{:S(2)}, u32[]{:S(2)}) async-start(bf16[32,136,128]{2,1,0:T(8,128)(2,1)} %get-tuple-element.11), calls=%async_computation | async-start | bytes 2228224 | tf_op jit(solution)/shard_map/all_to_all | solution.py:253
  23.0 2.2 %copy-start.5 = (bf16[32,1536]{1,0:T(8,128)(2,1)S(1)}, bf16[32,1536]{1,0:T(8,128)(2,1)}, u32[]{:S(2)}) copy-start(bf16[32,1536]{1,0:T(8,128)(2,1)} %param.16) | copy-start | bytes 294916
  23.0 29.6 %copy-start = (bf16[512,1024]{1,0:T(8,128)(2,1)S(1)}, bf16[512,1024]{1,0:T(8,128)(2,1)}, u32[]{:S(2)}) copy-start(bf16[512,1024]{1,0:T(8,128)(2,1)} %up_ref.1) | copy-start | bytes 3145732
  23.0 29.6 %copy-start.1 = (bf16[1024,512]{1,0:T(8,128)(2,1)S(1)}, bf16[1024,512]{1,0:T(8,128)(2,1)}, u32[]{:S(2)}) copy-start(bf16[1024,512]{1,0:T(8,128)(2,1)} %down_ref.1) | copy-start | bytes 3145732
  23.0 29.6 %copy-start.2 = (bf16[512,512]{1,0:T(8,128)(2,1)S(1)}, bf16[512,512]{1,0:T(8,128)(2,1)}, u32[]{:S(2)}) copy-start(bf16[512,512]{1,0:T(8,128)(2,1)} %cross_ref.1) | copy-start | bytes 1572868
  23.0 29.6 %copy-start.3 = (bf16[512,512]{1,0:T(8,128)(2,1)S(1)}, bf16[512,512]{1,0:T(8,128)(2,1)}, u32[]{:S(2)}) copy-start(bf16[512,512]{1,0:T(8,128)(2,1)} %refs_8_.1) | copy-start | bytes 1572868
  23.1 29.6 %copy-start.4 = (bf16[1,2,512]{2,1,0:T(2,128)(2,1)S(1)}, bf16[1,2,512]{2,1,0:T(2,128)(2,1)}, u32[]{:S(2)}) copy-start(bf16[1,2,512]{2,1,0:T(2,128)(2,1)} %param.10) | copy-start | bytes 6148
  25.2 13.3 %collective-permute-start.3 = (bf16[64,1536]{1,0:T(8,128)(2,1)S(1)}, bf16[64,1536]{1,0:T(8,128)(2,1)S(1)}, u32[]{:S(2)}, u32[]{:S(2)}) collective-permute-start(bf16[64,1536]{1,0:T(8,128)(2,1)S(1)} %constant_dynamic-update-slice_fusion.refs_0_), channel_id=1, source_target_pairs={{0,384},{32,416},{64,448},{96,480},{128,0},{160,32},{192,64},{224,... | collective-permute-start | bytes 589832 | tf_op jit(solution)/shard_map/ppermute | solution.py:265
  27.5 13.0 %collective-permute-start.2 = (bf16[64,1536]{1,0:T(8,128)(2,1)S(1)}, bf16[64,1536]{1,0:T(8,128)(2,1)}, u32[]{:S(2)}, u32[]{:S(2)}) collective-permute-start(bf16[64,1536]{1,0:T(8,128)(2,1)S(1)} %constant_dynamic-update-slice_fusion.refs_0_), channel_id=1, source_target_pairs={{0,64},{32,96},{64,128},{96,160},{128,192},{160,224},{192,256},{22... | collective-permute-start | bytes 589832 | tf_op jit(solution)/shard_map/ppermute | solution.py:267
  31.0 11.9 %collective-permute-start.1 = (bf16[64,1536]{1,0:T(8,128)(2,1)S(1)}, bf16[64,1536]{1,0:T(8,128)(2,1)}, u32[]{:S(2)}, u32[]{:S(2)}) collective-permute-start(bf16[64,1536]{1,0:T(8,128)(2,1)S(1)} %constant_dynamic-update-slice_fusion.refs_0_), channel_id=1, source_target_pairs={{0,448},{32,480},{64,0},{96,32},{128,64},{160,96},{192,128},{224,1... | collective-permute-start | bytes 589832 | tf_op jit(solution)/shard_map/ppermute | solution.py:266
  34.5 10.5 %collective-permute-start.4 = (bf16[64,1536]{1,0:T(8,128)(2,1)S(1)}, bf16[64,1536]{1,0:T(8,128)(2,1)}, u32[]{:S(2)}, u32[]{:S(2)}) collective-permute-start(bf16[64,1536]{1,0:T(8,128)(2,1)S(1)} %constant_dynamic-update-slice_fusion.refs_0_), channel_id=1, source_target_pairs={{0,32},{32,0},{64,96},{96,64},{128,160},{160,128},{192,224},{224,1... | collective-permute-start | bytes 589832 | tf_op jit(solution)/shard_map/ppermute | solution.py:269
  38.5 6.6 %collective-permute-start.7 = (bf16[64,1536]{1,0:T(8,128)(2,1)S(1)}, bf16[64,1536]{1,0:T(8,128)(2,1)}, u32[]{:S(2)}, u32[]{:S(2)}) collective-permute-start(bf16[64,1536]{1,0:T(8,128)(2,1)S(1)} %collective-permute-done.3.refs_3_), channel_id=1, source_target_pairs={{0,32},{32,0},{64,96},{96,64},{128,160},{160,128},{192,224},{224,1... | collective-permute-start | bytes 589832 | tf_op jit(solution)/shard_map/ppermute | solution.py:269
  40.4 4.6 %collective-permute-start.6 = (bf16[64,1536]{1,0:T(8,128)(2,1)}, bf16[64,1536]{1,0:T(8,128)(2,1)}, u32[]{:S(2)}, u32[]{:S(2)}) collective-permute-start(bf16[64,1536]{1,0:T(8,128)(2,1)} %collective-permute-done.2.refs_2_), channel_id=1, source_target_pairs={{0,32},{32,0},{64,96},{96,64},{128,160},{160,128},{192,224},{224,1... | collective-permute-start | bytes 589832 | tf_op jit(solution)/shard_map/ppermute | solution.py:269
  42.9 3.7 %collective-permute-start.5 = (bf16[64,1536]{1,0:T(8,128)(2,1)}, bf16[64,1536]{1,0:T(8,128)(2,1)}, u32[]{:S(2)}, u32[]{:S(2)}) collective-permute-start(bf16[64,1536]{1,0:T(8,128)(2,1)} %collective-permute-done.1.refs_1_), channel_id=1, source_target_pairs={{0,32},{32,0},{64,96},{96,64},{128,160},{160,128},{192,224},{224,1... | collective-permute-start | bytes 589832 | tf_op jit(solution)/shard_map/ppermute | solution.py:269
  67.8 33.2 %copy-start.6 = (bf16[512,1024]{1,0:T(8,128)(2,1)S(1)}, bf16[512,1024]{1,0:T(8,128)(2,1)}, u32[]{:S(2)}) copy-start(bf16[512,1024]{1,0:T(8,128)(2,1)} %pick_matrix.1) | copy-start | bytes 3145732
